TPU v7x, 128 devices: a whole 4x4x4 slice. The times are simulated.
128 devices in a mesh: ctx: 16 (over z, x), head: 8 (over y, core).
Axes of the slice: x: 4, y: 4, z: 4, core: 2. Of those that a mesh axis runs over, the one named last changes fastest.
Arguments:
- queries: bfloat16 [16384, 8192], P(('ctx', 'head')), may hold values from -200 to 200
- keys: bfloat16 [16384, 1024], P(('ctx', 'head')), may hold values from -6 to 6
- values: bfloat16 [16384, 1024], P(('ctx', 'head')), may hold values from -6 to 6
- out_grad: bfloat16 [16384, 8192], P(('ctx', 'head')), may hold values from -6 to 6
- doc_starts: int32 [256], replicated, may hold values from 0 to 16383, as said below
- piece_order: int32 [16, 16], replicated, may hold values from 0 to 15, as said below
Outputs:
- attended: bfloat16 [16384, 8192], P(('ctx', 'head'))
- query_grad: bfloat16 [16384, 8192], P(('ctx', 'head'))
- key_grad: bfloat16 [16384, 1024], P(('ctx', 'head'))
- value_grad: bfloat16 [16384, 1024], P(('ctx', 'head'))
Inputs may be any that keep to these rules, and one draw needn't show every extreme that they name: `doc_starts`: Increasing; the first is 0; every document, the last one running to 16384, has 1 to 256 tokens, and one has exactly 256. `piece_order`: row i names each of the 16 blocks of 64 consecutive tokens of context shard i once.
All inputs are finite; a program needn't handle non-finite values.
Results may differ from a plain program's by a relative error of at most 0.03.
Values may be sent and summed in bfloat16 or wider, within the bound.
A program may use at most 128 MiB of HBM per device.

v0:
```python
import math

import jax
import jax.numpy as jnp
from jax import lax
from jax.sharding import PartitionSpec as P

DH = 128
QBLK = 128
MOST = 256


def sign_grid(grid_size):
    row_ids = jnp.arange(grid_size, dtype=jnp.int32)[:, None]
    column_ids = jnp.arange(grid_size, dtype=jnp.int32)[None, :]
    common = jnp.bitwise_and(row_ids, column_ids)
    parity = jnp.zeros((grid_size, grid_size), jnp.int32)
    for shift_bit in range(grid_size.bit_length()):
        parity = parity + jnp.bitwise_and(jnp.right_shift(common, shift_bit), 1)
    return jnp.where(parity % 2 == 0, 1.0, -1.0).astype(jnp.float32)


def doc_begin(positions, doc_starts):
    flat_pos = positions.reshape(-1)
    before = doc_starts[None, :] <= flat_pos[:, None]
    begin_pos = jnp.max(jnp.where(before, doc_starts[None, :], 0), axis=1)
    return begin_pos.reshape(positions.shape)


def attend(queries_block, window, grads_block, query_pos, begin_pos, key_pos):
    inverse_root = 1.0 / math.sqrt(DH)
    pieces, query_rows, query_width = queries_block.shape
    window_rows = window.shape[1]
    key_width = window.shape[2] // 2
    key_heads = key_width // DH
    group_size = query_width // key_width
    key_part = window[:, :, :key_width].reshape(pieces, window_rows, key_heads, DH)
    value_part = window[:, :, key_width:].reshape(pieces, window_rows, key_heads, DH)
    query_split = queries_block.reshape(pieces, query_rows, key_heads, group_size, DH)
    grad_split = grads_block.reshape(pieces, query_rows, key_heads, group_size, DH)
    scores = (
        jnp.einsum("prhgd,pwhd->phgrw", query_split, key_part, preferred_element_type=jnp.float32)
        * inverse_root
    )
    allowed = (key_pos[:, None, :] <= query_pos[:, :, None]) & (
        key_pos[:, None, :] >= begin_pos[:, :, None]
    )
    allowed = allowed[:, None, None, :, :]
    masked = jnp.where(allowed, scores, -jnp.inf)
    row_top = jnp.max(masked, axis=-1, keepdims=True)
    row_total = jnp.sum(jnp.exp(masked - row_top), axis=-1, keepdims=True)
    logsum = row_top + jnp.log(row_total)
    probability = jnp.exp(masked - logsum)
    weights = probability.astype(jnp.bfloat16)
    output = jnp.einsum(
        "phgrw,pwhd->prhgd", weights, value_part, preferred_element_type=jnp.float32
    ).astype(jnp.bfloat16)
    row_delta = jnp.sum(grad_split.astype(jnp.float32) * output.astype(jnp.float32), axis=-1)
    row_delta = jnp.transpose(row_delta, (0, 2, 3, 1))[..., None]
    prob_grad = jnp.einsum(
        "prhgd,pwhd->phgrw", grad_split, value_part, preferred_element_type=jnp.float32
    )
    score_grad = (probability * (prob_grad - row_delta)).astype(jnp.bfloat16)
    query_term = (
        jnp.einsum("phgrw,pwhd->prhgd", score_grad, key_part, preferred_element_type=jnp.float32)
        * inverse_root
    )
    key_term = (
        jnp.einsum("phgrw,prhgd->pwhd", score_grad, query_split, preferred_element_type=jnp.float32)
        * inverse_root
    )
    value_term = jnp.einsum(
        "phgrw,prhgd->pwhd", weights, grad_split, preferred_element_type=jnp.float32
    )
    key_terms = jnp.concatenate(
        [
            key_term.reshape(pieces, window_rows, key_width),
            value_term.reshape(pieces, window_rows, key_width),
        ],
        axis=-1,
    )
    return (
        output.reshape(pieces, query_rows, query_width),
        query_term.reshape(pieces, query_rows, query_width),
        key_terms,
    )


def local(queries, keys, values, out_grad, doc_starts, piece_order):
    inverse_root = 1.0 / math.sqrt(DH)
    grid = sign_grid(DH)
    head_queries, head_keys, head_values, head_grads = (
        lax.all_to_all(queries, "head", split_axis=1, concat_axis=0, tiled=True),
        lax.all_to_all(keys, "head", split_axis=1, concat_axis=0, tiled=True),
        lax.all_to_all(values, "head", split_axis=1, concat_axis=0, tiled=True),
        lax.all_to_all(out_grad, "head", split_axis=1, concat_axis=0, tiled=True),
    )
    local_rows = head_queries.shape[0]
    query_width = head_queries.shape[1]
    key_width = head_keys.shape[1]
    shard_count = lax.axis_size("ctx")
    shard_index = lax.axis_index("ctx")
    total_rows = local_rows * shard_count
    piece_rows = local_rows // shard_count
    shard_ids = jnp.arange(shard_count, dtype=jnp.int32)
    order_row = jnp.sum(jnp.where(shard_ids[:, None] == shard_index, piece_order, 0), axis=0)
    order_column = jnp.sum(jnp.where(shard_ids[None, :] == shard_index, piece_order, 0), axis=1)
    inverse_row = jnp.sum(
        jnp.where(order_row[:, None] == shard_ids[None, :], shard_ids[:, None], 0), axis=0
    )
    key_codes = (
        jnp.dot(head_keys, grid.astype(jnp.bfloat16), preferred_element_type=jnp.float32)
        * inverse_root
    ).astype(jnp.bfloat16)
    key_pack = jnp.concatenate([key_codes, head_values], axis=1)

    def rotate_back(blocks_in):
        turned = (
            jnp.dot(
                blocks_in.reshape(-1, DH),
                grid,
                precision=lax.Precision.HIGHEST,
                preferred_element_type=jnp.float32,
            )
            * inverse_root
        )
        return turned.astype(jnp.bfloat16).reshape(blocks_in.shape)

    pieces = head_queries.reshape(shard_count, piece_rows, head_queries.shape[1])
    sending = jnp.take(pieces, order_row, axis=0)
    arrived = lax.all_to_all(sending, "ctx", split_axis=0, concat_axis=0, tiled=True)
    balanced_queries = arrived.reshape(local_rows, head_queries.shape[1])
    whole_keys = lax.all_gather(key_pack, "ctx", axis=0, tiled=True)
    piece_pos = (shard_ids * local_rows + order_column * piece_rows)[:, None] + jnp.arange(
        piece_rows, dtype=jnp.int32
    )[None, :]
    piece_queries = balanced_queries.reshape(shard_count, piece_rows, query_width)
    piece_grads = head_grads.reshape(shard_count, piece_rows, query_width)
    batch_size = max(1, QBLK // piece_rows)
    window_rows = MOST + piece_rows
    window_ids = jnp.arange(window_rows, dtype=jnp.int32)

    def take_window(start_row):
        return lax.dynamic_slice_in_dim(whole_keys, start_row, window_rows, 0)

    def visit(buffer, step_index):
        first_row = step_index * batch_size
        queries_block = lax.dynamic_slice_in_dim(piece_queries, first_row, batch_size, 0)
        grads_block = lax.dynamic_slice_in_dim(piece_grads, first_row, batch_size, 0)
        query_pos = lax.dynamic_slice_in_dim(piece_pos, first_row, batch_size, 0)
        window_start = jnp.maximum(query_pos[:, 0] - MOST, 0)
        window = jax.vmap(take_window)(window_start)
        key_pos = window_start[:, None] + window_ids[None, :]
        output, query_term, key_terms = attend(
            queries_block, window, grads_block, query_pos, doc_begin(query_pos, doc_starts), key_pos
        )

        def deposit(slot_index, gathered):
            start_row = window_start[slot_index]
            current = lax.dynamic_slice_in_dim(gathered, start_row, window_rows, 0)
            return lax.dynamic_update_slice_in_dim(
                gathered, current + key_terms[slot_index], start_row, 0
            )

        buffer = lax.fori_loop(0, batch_size, deposit, buffer)
        return (buffer, (output, query_term))

    start_buffer = jnp.zeros((total_rows, 2 * key_width), jnp.float32)
    buffer, (output, query_term) = lax.scan(
        visit, start_buffer, jnp.arange(shard_count // batch_size, dtype=jnp.int32)
    )
    attended = output.reshape(local_rows, query_width)
    blocks_in = rotate_back(query_term.reshape(local_rows, query_width))
    pieces = blocks_in.reshape(shard_count, piece_rows, blocks_in.shape[1])
    arrived = lax.all_to_all(pieces, "ctx", split_axis=0, concat_axis=0, tiled=True)
    query_grad = jnp.take(arrived, inverse_row, axis=0).reshape(local_rows, blocks_in.shape[1])
    summed_terms = lax.psum_scatter(buffer, "ctx", scatter_dimension=0, tiled=True)
    key_grad = rotate_back(summed_terms[:, :key_width])
    value_grad = summed_terms[:, key_width:].astype(jnp.bfloat16)
    return (
        lax.all_to_all(attended, "head", split_axis=0, concat_axis=1, tiled=True),
        lax.all_to_all(query_grad, "head", split_axis=0, concat_axis=1, tiled=True),
        lax.all_to_all(key_grad, "head", split_axis=0, concat_axis=1, tiled=True),
        lax.all_to_all(value_grad, "head", split_axis=0, concat_axis=1, tiled=True),
    )


def solution(mesh):
    return jax.shard_map(
        local,
        mesh=mesh,
        in_specs=(
            P(("ctx", "head"), None),
            P(("ctx", "head"), None),
            P(("ctx", "head"), None),
            P(("ctx", "head"), None),
            P(),
            P(),
        ),
        out_specs=(
            P(("ctx", "head"), None),
            P(("ctx", "head"), None),
            P(("ctx", "head"), None),
            P(("ctx", "head"), None),
        ),
        check_vma=False,
    )
```

profile of v0, /device:TPU:63, one launch (start us, length us, event | category | flops | bytes accessed | tf_op | source)
XLA Modules:
  0.0 487.4 jit_solution(4838376099060539574)
XLA Ops:
  18.8 6.1 %all-to-all-start.3 = ((bf16[128,8,128]{0,2,1:T(8,128)(2,1)}), bf16[128,8,128]{0,2,1:T(8,128)(2,1)S(1)}, u32[]{:S(2)}, u32[]{:S(2)}) async-start(bf16[128,8,128]{0,2,1:T(8,128)(2,1)} %bitcast.9), calls=%async_computation.3 | async-start | bytes 524288 | tf_op jit(solution)/shard_map/all_to_all | solution.py:95
  33.0 6.3 %all-to-all-start = ((bf16[128,8,1024]{0,2,1:T(8,128)(2,1)}), bf16[128,8,1024]{0,2,1:T(8,128)(2,1)S(1)}, u32[]{:S(2)}, u32[]{:S(2)}) async-start(bf16[128,8,1024]{0,2,1:T(8,128)(2,1)} %bitcast.237), calls=%async_computation | async-start | bytes 4194304 | tf_op jit(solution)/shard_map/all_to_all | solution.py:93
  42.5 21.4 %all-to-all-done = bf16[128,8,1024]{0,2,1:T(8,128)(2,1)S(1)} async-done(((bf16[128,8,1024]{0,2,1:T(8,128)(2,1)}), bf16[128,8,1024]{0,2,1:T(8,128)(2,1)S(1)}, u32[]{:S(2)}, u32[]{:S(2)}) %all-to-all-start) | async-done | bytes 2097184 | tf_op jit(solution)/shard_map/all_to_all | solution.py:93
  63.9 7.0 %all-to-all-start.4 = ((bf16[128,8,1024]{2,0,1:T(8,128)(2,1)}), bf16[128,8,1024]{2,0,1:T(8,128)(2,1)}, u32[]{:S(2)}, u32[]{:S(2)}) async-start(bf16[128,8,1024]{2,0,1:T(8,128)(2,1)} %bitcast.166), calls=%async_computation.4 | async-start | bytes 4194304 | tf_op jit(solution)/shard_map/all_to_all | solution.py:96
  77.6 18.0 %all-to-all-done.4 = bf16[128,8,1024]{2,0,1:T(8,128)(2,1)} async-done(((bf16[128,8,1024]{2,0,1:T(8,128)(2,1)}), bf16[128,8,1024]{2,0,1:T(8,128)(2,1)}, u32[]{:S(2)}, u32[]{:S(2)}) %all-to-all-start.4) | async-done | bytes 2097184 | tf_op jit(solution)/shard_map/all_to_all | solution.py:96
  95.6 7.3 %all-to-all-start.1 = ((bf16[16,64,1024]{2,1,0:T(8,128)(2,1)}), bf16[16,64,1024]{2,1,0:T(8,128)(2,1)}, u32[]{:S(2)}, u32[]{:S(2)}) async-start(bf16[16,64,1024]{2,1,0:T(8,128)(2,1)} %broadcast_select_fusion.1), calls=%async_computation.1 | async-start | bytes 4194304 | tf_op jit(solution)/shard_map/all_to_all | solution.py:131
  103.0 12.0 %copy.104 = bf16[16384,256]{1,0:T(8,128)(2,1)} copy(bf16[16384,256]{0,1:T(8,128)(2,1)} %all-gather.2.cloned.1.call-done) | data formatting | bytes 16777216
  115.0 13.8 %all-to-all-done.1 = bf16[16,64,1024]{2,1,0:T(8,128)(2,1)} async-done(((bf16[16,64,1024]{2,1,0:T(8,128)(2,1)}), bf16[16,64,1024]{2,1,0:T(8,128)(2,1)}, u32[]{:S(2)}, u32[]{:S(2)}) %all-to-all-start.1) | async-done | bytes 2097184 | tf_op jit(solution)/shard_map/all_to_all | solution.py:131
  128.7 6.0 %broadcast_in_dim.124 = f32[16384,256]{1,0:T(8,128)} broadcast(f32[]{:T(128)} %constant.134.clone.1), dimensions={} | broadcast | bytes 16777220 | tf_op jit(solution)/shard_map/broadcast_in_dim | solution.py:168
  134.7 179.0 %while.41 = (s32[]{:T(128)}, f32[16384,256]{1,0:T(8,128)}, bf16[8,2,64,1024]{3,2,1,0:T(8,128)(2,1)}, f32[8,2,64,1024]{3,2,1,0:T(8,128)}, s32[8]{0:T(128)S(1)}, /...) while((s32[]{:T(128)}, f32[16384,256]{1,0:T(8,128)}, ...), condition=%wide.region_9.11_spmd.clone, body=%wide.region_2.10_spmd.clone.sunk | while | flops 508123648 | bytes 23352432 | solution.py:169
  143.7 10.8 %while.43 = (s32[]{:T(128)}, f32[16384,256]{1,0:T(8,128)}, s32[2]{0:T(128)S(1)}, f32[2,320,256]{2,1,0:T(8,128)S(1)}, s32[]{:T(128)}, /*index=5*/s32[]{:T(128)}, s32[]{:T(128)}) while((s32[]{:T(128)}, f32[16384,256]{1,0:T(8,128)}, s32[2]{0:T(128)S(1)}, f32[2,320,256]{2,1,0:T(8,128)S(1)}, s32[]{:T(128)}, /*index=5*/s32[]{:T(128)}, ...), condition=%wide.region_8.9_spmd, body=%wide.region_7.8_spmd.sunk | while | flops 81925 | bytes 1638535 | solution.py:165
  166.1 10.8 %while.43 = (s32[]{:T(128)}, f32[16384,256]{1,0:T(8,128)}, s32[2]{0:T(128)S(1)}, f32[2,320,256]{2,1,0:T(8,128)S(1)}, s32[]{:T(128)}, /*index=5*/s32[]{:T(128)}, s32[]{:T(128)}) while((s32[]{:T(128)}, f32[16384,256]{1,0:T(8,128)}, s32[2]{0:T(128)S(1)}, f32[2,320,256]{2,1,0:T(8,128)S(1)}, s32[]{:T(128)}, /*index=5*/s32[]{:T(128)}, ...), condition=%wide.region_8.9_spmd, body=%wide.region_7.8_spmd.sunk | while | flops 81925 | bytes 1638535 | solution.py:165
  188.5 10.8 %while.43 = (s32[]{:T(128)}, f32[16384,256]{1,0:T(8,128)}, s32[2]{0:T(128)S(1)}, f32[2,320,256]{2,1,0:T(8,128)S(1)}, s32[]{:T(128)}, /*index=5*/s32[]{:T(128)}, s32[]{:T(128)}) while((s32[]{:T(128)}, f32[16384,256]{1,0:T(8,128)}, s32[2]{0:T(128)S(1)}, f32[2,320,256]{2,1,0:T(8,128)S(1)}, s32[]{:T(128)}, /*index=5*/s32[]{:T(128)}, ...), condition=%wide.region_8.9_spmd, body=%wide.region_7.8_spmd.sunk | while | flops 81925 | bytes 1638535 | solution.py:165
  210.8 10.8 %while.43 = (s32[]{:T(128)}, f32[16384,256]{1,0:T(8,128)}, s32[2]{0:T(128)S(1)}, f32[2,320,256]{2,1,0:T(8,128)S(1)}, s32[]{:T(128)}, /*index=5*/s32[]{:T(128)}, s32[]{:T(128)}) while((s32[]{:T(128)}, f32[16384,256]{1,0:T(8,128)}, s32[2]{0:T(128)S(1)}, f32[2,320,256]{2,1,0:T(8,128)S(1)}, s32[]{:T(128)}, /*index=5*/s32[]{:T(128)}, ...), condition=%wide.region_8.9_spmd, body=%wide.region_7.8_spmd.sunk | while | flops 81925 | bytes 1638535 | solution.py:165
  233.1 10.9 %while.43 = (s32[]{:T(128)}, f32[16384,256]{1,0:T(8,128)}, s32[2]{0:T(128)S(1)}, f32[2,320,256]{2,1,0:T(8,128)S(1)}, s32[]{:T(128)}, /*index=5*/s32[]{:T(128)}, s32[]{:T(128)}) while((s32[]{:T(128)}, f32[16384,256]{1,0:T(8,128)}, s32[2]{0:T(128)S(1)}, f32[2,320,256]{2,1,0:T(8,128)S(1)}, s32[]{:T(128)}, /*index=5*/s32[]{:T(128)}, ...), condition=%wide.region_8.9_spmd, body=%wide.region_7.8_spmd.sunk | while | flops 81925 | bytes 1638535 | solution.py:165
  255.6 10.8 %while.43 = (s32[]{:T(128)}, f32[16384,256]{1,0:T(8,128)}, s32[2]{0:T(128)S(1)}, f32[2,320,256]{2,1,0:T(8,128)S(1)}, s32[]{:T(128)}, /*index=5*/s32[]{:T(128)}, s32[]{:T(128)}) while((s32[]{:T(128)}, f32[16384,256]{1,0:T(8,128)}, s32[2]{0:T(128)S(1)}, f32[2,320,256]{2,1,0:T(8,128)S(1)}, s32[]{:T(128)}, /*index=5*/s32[]{:T(128)}, ...), condition=%wide.region_8.9_spmd, body=%wide.region_7.8_spmd.sunk | while | flops 81925 | bytes 1638535 | solution.py:165
  277.9 10.8 %while.43 = (s32[]{:T(128)}, f32[16384,256]{1,0:T(8,128)}, s32[2]{0:T(128)S(1)}, f32[2,320,256]{2,1,0:T(8,128)S(1)}, s32[]{:T(128)}, /*index=5*/s32[]{:T(128)}, s32[]{:T(128)}) while((s32[]{:T(128)}, f32[16384,256]{1,0:T(8,128)}, s32[2]{0:T(128)S(1)}, f32[2,320,256]{2,1,0:T(8,128)S(1)}, s32[]{:T(128)}, /*index=5*/s32[]{:T(128)}, ...), condition=%wide.region_8.9_spmd, body=%wide.region_7.8_spmd.sunk | while | flops 81925 | bytes 1638535 | solution.py:165
  300.3 10.8 %while.43 = (s32[]{:T(128)}, f32[16384,256]{1,0:T(8,128)}, s32[2]{0:T(128)S(1)}, f32[2,320,256]{2,1,0:T(8,128)S(1)}, s32[]{:T(128)}, /*index=5*/s32[]{:T(128)}, s32[]{:T(128)}) while((s32[]{:T(128)}, f32[16384,256]{1,0:T(8,128)}, s32[2]{0:T(128)S(1)}, f32[2,320,256]{2,1,0:T(8,128)S(1)}, s32[]{:T(128)}, /*index=5*/s32[]{:T(128)}, ...), condition=%wide.region_8.9_spmd, body=%wide.region_7.8_spmd.sunk | while | flops 81925 | bytes 1638535 | solution.py:165
  326.2 51.0 %all_to_all.156 = bf16[16,64,1024]{2,1,0:T(8,128)(2,1)} all-to-all(bf16[16,64,1024]{2,1,0:T(8,128)(2,1)} %reshape_reshape.7), channel_id=1, replica_groups=mesh['ctx'=16,'head'=8] {'ctx'}, dimensions={0} | all-to-all | bytes 4194304 | tf_op jit(solution)/shard_map/all_to_all | solution.py:175
  377.2 8.5 %all-to-all-start.5 = ((bf16[8,128,1024]{2,1,0:T(8,128)(2,1)}), bf16[8,128,1024]{2,1,0:T(8,128)(2,1)S(1)}, u32[]{:S(2)}, u32[]{:S(2)}) async-start(bf16[8,128,1024]{2,1,0:T(8,128)(2,1)} %bitcast.242), calls=%async_computation.5 | async-start | bytes 4194304 | tf_op jit(solution)/shard_map/all_to_all | solution.py:181
  392.7 17.6 %all-to-all-done.5 = bf16[8,128,1024]{2,1,0:T(8,128)(2,1)S(1)} async-done(((bf16[8,128,1024]{2,1,0:T(8,128)(2,1)}), bf16[8,128,1024]{2,1,0:T(8,128)(2,1)S(1)}, u32[]{:S(2)}, u32[]{:S(2)}) %all-to-all-start.5) | async-done | bytes 2097184 | tf_op jit(solution)/shard_map/all_to_all | solution.py:181
  410.3 6.8 %all-to-all-start.7 = ((bf16[8,128,1024]{2,1,0:T(8,128)(2,1)}), bf16[8,128,1024]{2,1,0:T(8,128)(2,1)}, u32[]{:S(2)}, u32[]{:S(2)}) async-start(bf16[8,128,1024]{2,1,0:T(8,128)(2,1)} %bitcast.236), calls=%async_computation.7 | async-start | bytes 4194304 | tf_op jit(solution)/shard_map/all_to_all | solution.py:182
  417.2 31.5 %reduce-scatter.2.cloned.1.call-done = f32[1024,256]{1,0:T(8,128)} async-done(((f32[16384,256]{1,0:T(8,128)}), f32[1024,256]{1,0:T(8,128)}) %reduce-scatter.2.cloned.1.call-update) | async-done | bytes 1048592 | tf_op jit(solution)/shard_map/reduce_scatter | solution.py:177
  460.3 6.1 %all-to-all-start.8 = ((bf16[8,128,128]{2,1,0:T(8,128)(2,1)}), bf16[8,128,128]{2,1,0:T(8,128)(2,1)S(1)}, u32[]{:S(2)}, u32[]{:S(2)}) async-start(bf16[8,128,128]{2,1,0:T(8,128)(2,1)} %bitcast.19), calls=%async_computation.9 | async-start | bytes 524288 | tf_op jit(solution)/shard_map/all_to_all | solution.py:183
  (377 shorter events, 232.3 us)
Async XLA Ops:
  9.0 9.8 %all-to-all-start.2 = ((bf16[128,8,128]{0,2,1:T(8,128)(2,1)}), bf16[128,8,128]{0,2,1:T(8,128)(2,1)S(1)}, u32[]{:S(2)}, u32[]{:S(2)}) async-start(bf16[128,8,128]{0,2,1:T(8,128)(2,1)} %bitcast.5), calls=%async_computation.2 | async-start | bytes 524288 | tf_op jit(solution)/shard_map/all_to_all | solution.py:94
  15.8 14.8 %copy-start = (bf16[128,8192]{1,0:T(8,128)(2,1)S(1)}, bf16[128,8192]{1,0:T(8,128)(2,1)}, u32[]{:S(2)}) copy-start(bf16[128,8192]{1,0:T(8,128)(2,1)} %param.12) | copy-start | bytes 6291460
  18.8 10.9 %all-to-all-start.3 = ((bf16[128,8,128]{0,2,1:T(8,128)(2,1)}), bf16[128,8,128]{0,2,1:T(8,128)(2,1)S(1)}, u32[]{:S(2)}, u32[]{:S(2)}) async-start(bf16[128,8,128]{0,2,1:T(8,128)(2,1)} %bitcast.9), calls=%async_computation.3 | async-start | bytes 524288 | tf_op jit(solution)/shard_map/all_to_all | solution.py:95
  24.9 78.1 %all-gather.2.cloned.1.call-start = ((), (), s32[]{:S(2)}) async-start(), calls=%async_computation.11 | async-start | bytes 8912896 | tf_op jit(solution)/shard_map/all_gather | solution.py:133
  33.0 30.9 %all-to-all-start = ((bf16[128,8,1024]{0,2,1:T(8,128)(2,1)}), bf16[128,8,1024]{0,2,1:T(8,128)(2,1)S(1)}, u32[]{:S(2)}, u32[]{:S(2)}) async-start(bf16[128,8,1024]{0,2,1:T(8,128)(2,1)} %bitcast.237), calls=%async_computation | async-start | bytes 4194304 | tf_op jit(solution)/shard_map/all_to_all | solution.py:93
  63.9 7.0 %copy-start.2 = (s32[16,16]{1,0:T(8,128)S(1)}, s32[16,16]{1,0:T(8,128)}, u32[]{:S(2)}) copy-start(s32[16,16]{1,0:T(8,128)} %param.17) | copy-start | bytes 3076
  63.9 31.7 %all-to-all-start.4 = ((bf16[128,8,1024]{2,0,1:T(8,128)(2,1)}), bf16[128,8,1024]{2,0,1:T(8,128)(2,1)}, u32[]{:S(2)}, u32[]{:S(2)}) async-start(bf16[128,8,1024]{2,0,1:T(8,128)(2,1)} %bitcast.166), calls=%async_computation.4 | async-start | bytes 4194304 | tf_op jit(solution)/shard_map/all_to_all | solution.py:96
  95.6 33.1 %all-to-all-start.1 = ((bf16[16,64,1024]{2,1,0:T(8,128)(2,1)}), bf16[16,64,1024]{2,1,0:T(8,128)(2,1)}, u32[]{:S(2)}, u32[]{:S(2)}) async-start(bf16[16,64,1024]{2,1,0:T(8,128)(2,1)} %broadcast_select_fusion.1), calls=%async_computation.1 | async-start | bytes 4194304 | tf_op jit(solution)/shard_map/all_to_all | solution.py:131
  102.8 345.9 %reduce-scatter.2.cloned.1.call-start = ((), (), s32[]{:S(2)}) async-start(), calls=%async_computation.12 | async-start | bytes 17825792 | tf_op jit(solution)/shard_map/reduce_scatter | solution.py:177
  128.7 6.0 %copy-start.1 = (s32[256]{0:T(256)S(1)}, s32[256]{0:T(256)}, u32[]{:S(2)}) copy-start(s32[256]{0:T(256)} %param.16) | copy-start | bytes 3076
  377.2 33.1 %all-to-all-start.5 = ((bf16[8,128,1024]{2,1,0:T(8,128)(2,1)}), bf16[8,128,1024]{2,1,0:T(8,128)(2,1)S(1)}, u32[]{:S(2)}, u32[]{:S(2)}) async-start(bf16[8,128,1024]{2,1,0:T(8,128)(2,1)} %bitcast.242), calls=%async_computation.5 | async-start | bytes 4194304 | tf_op jit(solution)/shard_map/all_to_all | solution.py:181
  410.3 40.2 %all-to-all-start.7 = ((bf16[8,128,1024]{2,1,0:T(8,128)(2,1)}), bf16[8,128,1024]{2,1,0:T(8,128)(2,1)}, u32[]{:S(2)}, u32[]{:S(2)}) async-start(bf16[8,128,1024]{2,1,0:T(8,128)(2,1)} %bitcast.236), calls=%async_computation.7 | async-start | bytes 4194304 | tf_op jit(solution)/shard_map/all_to_all | solution.py:182
  450.5 9.8 %all-to-all-start.9 = ((bf16[8,128,128]{2,1,0:T(8,128)(2,1)}), bf16[8,128,128]{2,1,0:T(8,128)(2,1)S(1)}, u32[]{:S(2)}, u32[]{:S(2)}) async-start(bf16[8,128,128]{2,1,0:T(8,128)(2,1)} %bitcast.21), calls=%async_computation.10 | async-start | bytes 524288 | tf_op jit(solution)/shard_map/all_to_all | solution.py:184
  460.3 19.5 %all-to-all-start.8 = ((bf16[8,128,128]{2,1,0:T(8,128)(2,1)}), bf16[8,128,128]{2,1,0:T(8,128)(2,1)S(1)}, u32[]{:S(2)}, u32[]{:S(2)}) async-start(bf16[8,128,128]{2,1,0:T(8,128)(2,1)} %bitcast.19), calls=%async_computation.9 | async-start | bytes 524288 | tf_op jit(solution)/shard_map/all_to_all | solution.py:183
Sparse Core Ops, SparseCore 0:
  30.7 71.3 all-gather.1
  313.8 134.8 reduce-scatter.1
where the time goes:
time: 494 us; the launch traced here: 487 us
  local copies, waits for them, and re-layouts  148 us (30%)
  waiting for transfers between devices  112 us (23%)
  starting transfers between devices  58.2 us (12%)
  blocking collectives  51 us (10%)
  loops' own time  38.1 us (8%)
  other arithmetic  34 us (7%)
  matrix products  32.3 us (7%)
  between operations  14.2 us (3%)
    all_to_all x1, blocking collectives, local(): lax.all_to_all(pieces, 'ctx', split_axis=0, concat_axis=0, tiled=True)  51 us
    reduce_scatter x1, waiting for transfers between devices, local(): lax.psum_scatter(buffer, 'ctx', scatter_dimension=0, tiled=True)  31.5 us
    another operation x8, loops' own time, visit(): buffer = lax.fori_loop(0, batch_size, deposit, buffer)  31.3 us
    dynamic_update_slice x16, local copies, waits for them, and re-layouts, deposit(): lax.dynamic_update_slice_in_dim(gathered, current + key_terms[slot_index]...  29.5 us
    unnamed x13, local copies, waits for them, and re-layouts  25.8 us
    all_to_all x1, waiting for transfers between devices, local(): lax.all_to_all(queries, 'head', split_axis=1, concat_axis=0, tiled=True)  21.4 us
    all_to_all x1, waiting for transfers between devices, local(): lax.all_to_all(out_grad, 'head', split_axis=1, concat_axis=0, tiled=True)  18 us
    all_to_all x1, waiting for transfers between devices, local(): lax.all_to_all(attended, 'head', split_axis=0, concat_axis=1, tiled=True)  17.6 us
  transfers between devices with their start and end apart: 11, of which 8 were waited for; matrix products, arithmetic and copies ran while one was open for 13% of the time, Pallas kernels for 0%

commit v1 on v0

v1 whole, which is shorter than its diff:
```python
import functools
import math

import jax
import jax.numpy as jnp
import numpy as np
from jax import lax
from jax.experimental import pallas as pl
from jax.experimental.pallas import tpu as pltpu
from jax.sharding import PartitionSpec as P

MESH = pl.DeviceIdType.MESH
DH = 128
BLK = 128
MOST = 256
WIN = MOST + BLK
PIECE = 64
SHARD = 1024
WIDE = 1024
NCTX = 16
NHEAD = 8
GROUP = 2
NEG = -1e30
ROOT = 1.0 / math.sqrt(DH)


def sign_grid():
    ids = np.arange(DH)
    common = ids[:, None] & ids[None, :]
    parity = np.zeros((DH, DH), np.int64)
    for bit in range(8):
        parity += (common >> bit) & 1
    return np.where(parity % 2 == 0, 1.0, -1.0).astype(np.float32)


def unit(shard, kv):
    even = kv % 2 == 0
    return (
        jnp.where(even, shard, (kv // 2) * 4 + shard % 4),
        jnp.where(even, kv, 2 * (shard // 4) + 1),
    )


def attention_kernel(
    q, k, v, g, docs, order, sign,
    att_o, qg_o, kg_o, vg_o,
    qbuf, qrel, kraw, kcod, vbuf, gbuf, pst, att, stg, arel, dqs, dk, dv, hk, hv, kst, vst,
    s_k, s_v, s_hk, s_hv, s_qr, s_qo, s_qa, s_qf, s_g, s_att, s_af, s_qg, s_kg, s_vg, s_hal,
    r_k, r_v, r_q, r_qrel, r_g, r_arel, r_att, r_qg, r_kg, r_vg, r_hal,
):
    c = lax.axis_index("ctx")
    h = lax.axis_index("head")
    z, x, y, co = c // 4, c % 4, h // 2, h % 2
    shard = jnp.where(co == 0, c, y * 4 + x)
    kv = jnp.where(co == 0, 2 * y, 2 * z + 1)

    def al(index, size):
        return pl.ds(pl.multiple_of(index * size, size), size)

    def start(copy):
        src, dst, ssem, rsem, tc, th = copy
        own = (tc == c) & (th == h)

        @pl.when(own)
        def _():
            pltpu.make_async_copy(src, dst, rsem).start()

        @pl.when(jnp.logical_not(own))
        def _():
            pltpu.make_async_remote_copy(
                src, dst, ssem, rsem, device_id={"ctx": tc, "head": th}, device_id_type=MESH
            ).start()

    def drain(copy):
        src, dst, ssem, rsem, tc, th = copy
        own = (tc == c) & (th == h)

        @pl.when(jnp.logical_not(own))
        def _():
            pltpu.make_async_remote_copy(
                src, dst, ssem, rsem, device_id={"ctx": tc, "head": th}, device_id_type=MESH
            ).wait_send()

    def landed(ref, sem):
        pltpu.make_async_copy(ref, ref, sem).wait()

    def loop(count, body):
        def step(s, carry):
            body(s)
            return carry

        lax.fori_loop(0, count, step, 0)

    def copy_k(s):
        kk = (h + s) % NHEAD
        return (k.at[:, al(kk, DH)], kraw.at[al(h + 2, BLK)], s_k.at[s], r_k.at[h + 2]) + unit(c, kk)

    def copy_v(s):
        kk = (h + s) % NHEAD
        return (v.at[:, al(kk, DH)], vbuf.at[al(h + 2, BLK)], s_v.at[s], r_v.at[h + 2]) + unit(c, kk)

    def copy_hk(s):
        kk = (h + s) % NHEAD
        slot = kraw.at[al(h % 2, BLK)]
        return (k.at[:, al(kk, DH)], slot, s_hk.at[s], r_k.at[h % 2]) + unit((c + 1) % NCTX, kk)

    def copy_hv(s):
        kk = (h + s) % NHEAD
        slot = vbuf.at[al(h % 2, BLK)]
        return (v.at[:, al(kk, DH)], slot, s_hv.at[s], r_v.at[h % 2]) + unit((c + 1) % NCTX, kk)

    def copy_qr(s):
        to = (z + s + 1) % 4
        return (q.at[:, al(2 * to + 1, WIDE)], qrel.at[z], s_qr.at[s], r_qrel.at[z], to * 4 + x, h)

    def copy_qo():
        return (q.at[:, al(2 * z + 1, WIDE)], qbuf.at[h], s_qo.at[0], r_q.at[h], c, 2 * z + 1)

    def copy_qa(s):
        to = 2 * ((y + s) % 4)
        return (q.at[:, al(to, WIDE)], qbuf.at[h], s_qa.at[s], r_q.at[h], c, to)

    def copy_qf(s):
        src = (z + 3 - s) % 4
        return (qrel.at[src], qbuf.at[h], s_qf.at[s], r_q.at[h], c, 2 * src + 1)

    def copy_g(s):
        half = s % 2
        kk = (h + s // 2) % NHEAD
        src = g.at[al(half, PIECE), al(kk, WIDE)]
        return (src, gbuf.at[c], s_g.at[s], r_g.at[c]) + unit(2 * h + half, kk)

    def copy_att_far(s):
        j = (c + s) % NCTX
        slot = z * 2 + x % 2
        return (stg.at[j], arel.at[slot], s_att.at[s], r_arel.at[slot], j, 2 * y + x // 2)

    def copy_att_near(s):
        j = (c + s) % NCTX
        dst = att_o.at[al(x % 2, PIECE), al(kv, WIDE)]
        return (stg.at[j], dst, s_att.at[s], r_att.at[(x % 2) * 8 + kv], j, 2 * y + x // 2)

    def relayed(s):
        return ((z + 4 - s // 2) % 4) * 2 + s % 2

    def copy_af(s):
        m = relayed(s)
        dst = att_o.at[al(m % 2, PIECE), al(2 * y, WIDE)]
        return (arel.at[m], dst, s_af.at[s], r_att.at[(m % 2) * 8 + 2 * y], c, 2 * (m // 2) + co)

    def copy_qg(b):
        return (dqs.at[b], qg_o.at[:, al(kv, WIDE)], s_qg.at[b], r_qg.at[kv], shard, b)

    def copy_kg(b):
        return (kst.at[b], kg_o.at[:, al(kv, DH)], s_kg.at[b], r_kg.at[kv], shard, b)

    def copy_vg(b):
        return (vst.at[b], vg_o.at[:, al(kv, DH)], s_vg.at[b], r_vg.at[kv], shard, b)

    back = unit((shard + NCTX - 1) % NCTX, kv)
    copy_hal_k = (dk.at[pl.ds(0, MOST)], hk, s_hal.at[0], r_hal.at[0]) + back
    copy_hal_v = (dv.at[pl.ds(0, MOST)], hv, s_hal.at[1], r_hal.at[1]) + back

    def send_kv(s):
        start(copy_k(s))
        start(copy_v(s))

    def send_edge(s):
        start(copy_hk(s))
        start(copy_hv(s))

    loop(8, send_kv)

    @pl.when(h >= 6)
    def _():
        loop(8, send_edge)

    loop(3, lambda s: start(copy_qr(s)))
    start(copy_qo())
    loop(4, lambda s: start(copy_qa(s)))
    loop(16, lambda s: start(copy_g(s)))

    def pass_on(s):
        src = (z + 3 - s) % 4
        landed(qrel.at[src], r_qrel.at[src])
        start(copy_qf(s))

    loop(3, pass_on)

    dk[...] = jnp.zeros_like(dk)
    dv[...] = jnp.zeros_like(dv)
    starts = docs[...].astype(jnp.float32)

    loop(8, lambda b: landed(qbuf.at[b], r_q.at[b]))
    loop(16, lambda j: landed(gbuf.at[j], r_g.at[j]))
    loop(10, lambda n: landed(kraw.at[al(n, BLK)], r_k.at[n]))
    loop(10, lambda n: landed(vbuf.at[al(n, BLK)], r_v.at[n]))
    turned = jnp.dot(kraw[...], sign[...].astype(jnp.bfloat16), preferred_element_type=jnp.float32)
    kcod[...] = (turned * ROOT).astype(jnp.bfloat16)

    def pair(block, p):
        parts = [block[:, (GROUP * p + n) * DH : (GROUP * p + n + 1) * DH] for n in range(GROUP)]
        return jnp.concatenate(parts, axis=0)

    dims_nt = (((1,), (1,)), ((), ()))
    dims_tn = (((0,), (0,)), ((), ()))

    def forward(s):
        b = (h + 8 - s) % NHEAD
        row = lax.broadcasted_iota(jnp.int32, (BLK, 1), 0) + (shard * SHARD + b * BLK)
        rowf = row.astype(jnp.float32)
        begin = jnp.max(jnp.where(starts <= rowf, starts, 0.0), axis=1, keepdims=True)
        col = lax.broadcasted_iota(jnp.int32, (BLK, WIN), 1) + (shard * SHARD + b * BLK - MOST)
        colf = col.astype(jnp.float32)
        bias = jnp.where((colf <= rowf) & (colf >= begin), 0.0, NEG)
        bias = jnp.concatenate([bias] * GROUP, axis=0)
        kwin = kcod[pl.ds(pl.multiple_of(b * BLK, BLK), WIN), :]
        vwin = vbuf[pl.ds(pl.multiple_of(b * BLK, BLK), WIN), :]
        for p in range(8 // GROUP):
            q2 = jnp.concatenate(
                [qbuf[b, :, (GROUP * p + n) * DH : (GROUP * p + n + 1) * DH] for n in range(GROUP)], axis=0
            )
            score = lax.dot_general(q2, kwin, dims_nt, preferred_element_type=jnp.float32)
            score = score * (ROOT * math.log2(math.e)) + bias
            top = jnp.max(score, axis=1, keepdims=True)
            e = jnp.exp2(score - top)
            total = jnp.sum(e, axis=1, keepdims=True)
            w = (e * (1.0 / total)).astype(jnp.bfloat16)
            pst[b, p] = w
            out = jnp.dot(w, vwin, preferred_element_type=jnp.float32).astype(jnp.bfloat16)
            for n in range(GROUP):
                lanes = slice((GROUP * p + n) * DH, (GROUP * p + n + 1) * DH)
                att[2 * b, :, lanes] = out[n * BLK : n * BLK + PIECE]
                att[2 * b + 1, :, lanes] = out[n * BLK + PIECE : (n + 1) * BLK]

    loop(8, forward)

    def fill(j):
        stg[j] = att[order[shard, j]]

    loop(16, fill)

    def send_att(s):
        @pl.when(co == 0)
        def _():
            start(copy_att_far(s))

        @pl.when(co == 1)
        def _():
            start(copy_att_near(s))

    loop(16, send_att)

    def where_from(piece):
        def look(j, found):
            return jnp.where(order[shard, j] == piece, j, found)

        return lax.fori_loop(0, NCTX, look, 0)

    def backward(s):
        b = (h + s) % NHEAD
        j0 = where_from(2 * b)
        j1 = where_from(2 * b + 1)
        rows = pl.ds(pl.multiple_of(b * BLK, BLK), WIN)
        kwin = kraw[rows, :]
        vwin = vbuf[rows, :]
        dk_sum = jnp.zeros((WIN, DH), jnp.float32)
        dv_sum = jnp.zeros((WIN, DH), jnp.float32)
        for p in range(8 // GROUP):
            q_parts, g_parts, o_parts = [], [], []
            for n in range(GROUP):
                lanes = slice((GROUP * p + n) * DH, (GROUP * p + n + 1) * DH)
                q_parts.append(qbuf[b, :, lanes])
                g_parts += [gbuf[j0, :, lanes], gbuf[j1, :, lanes]]
                o_parts += [att[2 * b, :, lanes], att[2 * b + 1, :, lanes]]
            q2 = jnp.concatenate(q_parts, axis=0)
            g2 = jnp.concatenate(g_parts, axis=0)
            o2 = jnp.concatenate(o_parts, axis=0)
            delta = jnp.sum(g2.astype(jnp.float32) * o2.astype(jnp.float32), axis=1, keepdims=True)
            dprob = lax.dot_general(g2, vwin, dims_nt, preferred_element_type=jnp.float32)
            w = pst[b, p]
            ds = (w.astype(jnp.float32) * (dprob - delta)).astype(jnp.bfloat16)
            dq = (jnp.dot(ds, kwin, preferred_element_type=jnp.float32) * ROOT).astype(jnp.bfloat16)
            dk_sum += lax.dot_general(ds, q2, dims_tn, preferred_element_type=jnp.float32)
            dv_sum += lax.dot_general(w, g2, dims_tn, preferred_element_type=jnp.float32)
            for n in range(GROUP):
                lanes = slice((GROUP * p + n) * DH, (GROUP * p + n + 1) * DH)
                dqs[b, :, lanes] = dq[n * BLK : (n + 1) * BLK]
        dk[rows, :] += dk_sum
        dv[rows, :] += dv_sum

    def pass_att(s):
        m = relayed(s)
        landed(arel.at[m], r_arel.at[m])
        start(copy_af(s))

    loop(8, backward)
    loop(8, pass_att)
    loop(8, lambda b: start(copy_qg(b)))

    start(copy_hal_k)
    start(copy_hal_v)

    def finish(b, k_more=0.0, v_more=0.0):
        rows = al(b + 2, BLK)
        back_turned = jnp.dot(
            (dk[rows, :] + k_more) * ROOT,
            sign[...],
            precision=lax.Precision.HIGHEST,
            preferred_element_type=jnp.float32,
        )
        kst[b] = (back_turned * ROOT).astype(jnp.bfloat16)
        vst[b] = (dv[rows, :] + v_more).astype(jnp.bfloat16)

    loop(6, finish)
    landed(hk, r_hal.at[0])
    landed(hv, r_hal.at[1])
    loop(2, lambda n: finish(n + 6, hk[al(n, BLK), :], hv[al(n, BLK), :]))

    def send_kvg(b):
        start(copy_kg(b))
        start(copy_vg(b))

    loop(8, send_kvg)

    def drain_kv(s):
        drain(copy_k(s))
        drain(copy_v(s))

    def drain_edge(s):
        drain(copy_hk(s))
        drain(copy_hv(s))

    loop(8, drain_kv)

    @pl.when(h >= 6)
    def _():
        loop(8, drain_edge)

    loop(3, lambda s: drain(copy_qr(s)))
    drain(copy_qo())
    loop(4, lambda s: drain(copy_qa(s)))
    loop(3, lambda s: drain(copy_qf(s)))
    loop(16, lambda s: drain(copy_g(s)))

    @pl.when(co == 0)
    def _():
        loop(16, lambda s: drain(copy_att_far(s)))

    @pl.when(co == 1)
    def _():
        loop(16, lambda s: drain(copy_att_near(s)))

    loop(8, lambda s: drain(copy_af(s)))
    loop(8, lambda b: drain(copy_qg(b)))
    loop(8, lambda b: drain(copy_kg(b)))
    loop(8, lambda b: drain(copy_vg(b)))
    drain(copy_hal_k)
    drain(copy_hal_v)
    def due(n):
        landed(qg_o.at[:, al(n, WIDE)], r_qg.at[n])
        landed(kg_o.at[:, al(n, DH)], r_kg.at[n])
        landed(vg_o.at[:, al(n, DH)], r_vg.at[n])

    loop(16, lambda n: landed(att_o.at[al(n // 8, PIECE), al(n % 8, WIDE)], r_att.at[n]))
    loop(8, due)


def copy_kernel(*refs):
    for src, dst in zip(refs[:4], refs[4:]):
        dst[...] = src[...]


def local(queries, keys, values, out_grad, doc_starts, piece_order):
    any_spec = pl.BlockSpec(memory_space=pl.ANY)
    vmem = pl.BlockSpec(memory_space=pltpu.VMEM)
    smem = pl.BlockSpec(memory_space=pltpu.SMEM)
    bf, f32 = jnp.bfloat16, jnp.float32
    shapes = [
        jax.ShapeDtypeStruct(a.shape, bf) for a in (out_grad, queries, keys, values)
    ]
    dma = pltpu.SemaphoreType.DMA
    ext = SHARD + MOST
    results = pl.pallas_call(
        attention_kernel,
        out_shape=shapes,
        in_specs=[any_spec] * 4 + [vmem, smem, vmem],
        out_specs=[any_spec] * 4,
        scratch_shapes=[
            pltpu.VMEM((NHEAD, BLK, WIDE), bf),
            pltpu.VMEM((4, BLK, WIDE), bf),
            pltpu.VMEM((ext, DH), bf),
            pltpu.VMEM((ext, DH), bf),
            pltpu.VMEM((ext, DH), bf),
            pltpu.VMEM((NCTX, PIECE, WIDE), bf),
            pltpu.VMEM((NHEAD, 8 // GROUP, GROUP * BLK, WIN), bf),
            pltpu.VMEM((NCTX, PIECE, WIDE), bf),
            pltpu.VMEM((NCTX, PIECE, WIDE), bf),
            pltpu.VMEM((8, PIECE, WIDE), bf),
            pltpu.VMEM((NHEAD, BLK, WIDE), bf),
            pltpu.VMEM((ext, DH), f32),
            pltpu.VMEM((ext, DH), f32),
            pltpu.VMEM((MOST, DH), f32),
            pltpu.VMEM((MOST, DH), f32),
            pltpu.VMEM((NHEAD, BLK, DH), bf),
            pltpu.VMEM((NHEAD, BLK, DH), bf),
        ]
        + [dma((n,)) for n in (8, 8, 8, 8, 3, 1, 4, 3, 16, 16, 8, 8, 8, 8, 2)]
        + [dma((n,)) for n in (10, 10, 8, 4, 16, 8, 16, 8, 8, 8, 2)],
        compiler_params=pltpu.CompilerParams(
            has_side_effects=True, vmem_limit_bytes=48 * 1024 * 1024
        ),
        name="attention",
    )(
        queries, keys, values, out_grad,
        doc_starts.reshape(1, -1), piece_order, jnp.asarray(sign_grid()),
    )
    blocks = [pl.BlockSpec((PIECE // 4, a.shape[1]), lambda n: (n, 0)) for a in shapes]
    return tuple(
        pl.pallas_call(
            copy_kernel,
            grid=(8,),
            out_shape=shapes,
            in_specs=blocks,
            out_specs=blocks,
            name="place",
        )(*results)
    )


def solution(mesh):
    rows = P(("ctx", "head"), None)
    return jax.shard_map(
        local,
        mesh=mesh,
        in_specs=(rows, rows, rows, rows, P(), P()),
        out_specs=(rows, rows, rows, rows),
        check_vma=False,
    )
```

time: 494 us -> 171 us (0.35)
  the two profiles are of different devices: /device:TPU:63 before, /device:TPU:17 now
where the time goes in v1:
time: 171 us; the launch traced here: 170 us
  Pallas kernels  161 us (94%)
  local copies, waits for them, and re-layouts  8.17 us (5%)
    pallas_call x1, Pallas kernels, local(): pl.pallas_call(attention_kernel, out_shape=shapes, in_specs=[any_spec] *...  155 us
    unnamed x18, local copies, waits for them, and re-layouts  8.17 us
    pallas_call x1, Pallas kernels, local(): pl.pallas_call(copy_kernel, grid=(8,), out_shape=shapes, in_specs=blocks,...  6.65 us

profile of v1, /device:TPU:17, one launch (start us, length us, event | category | flops | bytes accessed | tf_op | source)
XLA Modules:
  0.0 170.2 jit_solution(5315447484251826858)
XLA Ops:
  0.6 0.0 copy-start.4
  0.6 0.9 copy-done.4
  1.6 0.0 copy-start.5
  1.6 0.9 copy-done.5
  2.5 0.0 copy-start.6
  2.5 0.8 copy-done.6
  3.4 0.0 copy-start.7
  3.4 0.7 copy-done.7
  4.1 0.0 copy-start.8
  4.1 0.7 copy-done.8
  4.8 154.7 %attention.1 = (bf16[128,8192]{1,0:T(8,128)(2,1)S(1)}, bf16[128,8192]{1,0:T(8,128)(2,1)S(1)}, bf16[128,1024]{1,0:T(8,128)(2,1)S(1)}, bf16[128,1024]{1,0:T(8,128)(2,1)S(1)}) custom-call(bf16[128,8192]{1,0:T(8,128)(2,1)} %q.1, bf16[128,1024]{1,0:T(8,128)(2,1)S(1)} %copy-done.4, bf16[128,1024]{1,0:T(8,128)(2,1)S(1)} %copy-done.5, bf16[128,8192]{1,0:T(8,128)(2,1)} %g.1, ...), custom_call_target="tpu_custom_call" | custom-call | tf_op jit(solution)/shard_map/attention/pallas_call | solution.py:384
  159.5 0.0 copy-start
  159.5 1.3 copy-done
  160.8 0.0 copy-start.1
  160.8 1.3 copy-done.1
  162.2 0.0 copy-start.2
  162.2 0.7 copy-done.2
  162.9 0.0 copy-start.3
  162.9 0.7 copy-done.3
  163.6 6.7 %place.1 = (bf16[128,8192]{1,0:T(8,128)(2,1)}, bf16[128,8192]{1,0:T(8,128)(2,1)}, bf16[128,1024]{1,0:T(8,128)(2,1)}, bf16[128,1024]{1,0:T(8,128)(2,1)}) custom-call(bf16[128,8192]{1,0:T(8,128)(2,1)} %copy-done, bf16[128,8192]{1,0:T(8,128)(2,1)} %copy-done.1, bf16[128,1024]{1,0:T(8,128)(2,1)} %copy-done.2, bf16[128,1024]{1,0:T(8,128)(2,1)} %copy-done.3), custom_call_target="tpu_custom_call" | custom-call | tf_op jit(solution)/shard_map/place/pallas_call | solution.py:420
Async XLA Ops:
  0.6 1.0 copy-start.4
  1.6 0.9 copy-start.5
  2.5 0.8 copy-start.6
  3.4 0.7 copy-start.7
  4.1 0.7 copy-start.8
  159.5 1.3 copy-start
  160.8 1.3 copy-start.1
  162.2 0.7 copy-start.2
  162.9 0.7 copy-start.3

commit v2 on v1

--- a/solution.py
+++ b/solution.py
@@ -44,9 +44,9 @@
 def attention_kernel(
     q, k, v, g, docs, order, sign,
     att_o, qg_o, kg_o, vg_o,
-    qbuf, qrel, kraw, kcod, vbuf, gbuf, pst, att, stg, arel, dqs, dk, dv, hk, hv, kst, vst,
-    s_k, s_v, s_hk, s_hv, s_qr, s_qo, s_qa, s_qf, s_g, s_att, s_af, s_qg, s_kg, s_vg, s_hal,
-    r_k, r_v, r_q, r_qrel, r_g, r_arel, r_att, r_qg, r_kg, r_vg, r_hal,
+    qbuf, qrel, kvin, kvs, kvrel, kvbuf, kraw, kcod, vbuf, gbuf, pst, att, stg, arel, dqs, dk, dv, hk, hv, kst, vst,
+    l_kv, s_kvr, s_kvo, s_kva, s_kvf, s_edge, s_qr, s_qo, s_qa, s_qf, s_g, s_att, s_af, s_qg, s_kg, s_vg, s_hal,
+    r_kv, r_kvrel, r_q, r_qrel, r_g, r_arel, r_att, r_qg, r_kg, r_vg, r_hal,
 ):
     c = lax.axis_index("ctx")
     h = lax.axis_index("head")
@@ -91,26 +91,30 @@
 
         lax.fori_loop(0, count, step, 0)
 
-    def copy_k(s):
+    def far(s):
+        return (z + 8 - y - s) % 4
+
+    def copy_kvr(s):
+        to = far(s)
+        return (kvs.at[2 * to + 1], kvrel.at[z], s_kvr.at[s], r_kvrel.at[z], to * 4 + x, h)
+
+    def copy_kvo():
+        return (kvs.at[2 * z + 1], kvbuf.at[h + 2], s_kvo.at[0], r_kv.at[h + 2], c, 2 * z + 1)
+
+    def copy_kva(s):
+        to = 2 * ((y + s) % 4)
+        return (kvs.at[to], kvbuf.at[h + 2], s_kva.at[s], r_kv.at[h + 2], c, to)
+
+    def copy_kvf(s):
+        src = (y + z + s) % 4
+        return (kvrel.at[src], kvbuf.at[h + 2], s_kvf.at[s], r_kv.at[h + 2], c, 2 * src + 1)
+
+    def copy_edge(s):
         kk = (h + s) % NHEAD
-        return (k.at[:, al(kk, DH)], kraw.at[al(h + 2, BLK)], s_k.at[s], r_k.at[h + 2]) + unit(c, kk)
-
-    def copy_v(s):
-        kk = (h + s) % NHEAD
-        return (v.at[:, al(kk, DH)], vbuf.at[al(h + 2, BLK)], s_v.at[s], r_v.at[h + 2]) + unit(c, kk)
-
-    def copy_hk(s):
-        kk = (h + s) % NHEAD
-        slot = kraw.at[al(h % 2, BLK)]
-        return (k.at[:, al(kk, DH)], slot, s_hk.at[s], r_k.at[h % 2]) + unit((c + 1) % NCTX, kk)
-
-    def copy_hv(s):
-        kk = (h + s) % NHEAD
-        slot = vbuf.at[al(h % 2, BLK)]
-        return (v.at[:, al(kk, DH)], slot, s_hv.at[s], r_v.at[h % 2]) + unit((c + 1) % NCTX, kk)
+        return (kvs.at[kk], kvbuf.at[h % 2], s_edge.at[s], r_kv.at[h % 2]) + unit((c + 1) % NCTX, kk)
 
     def copy_qr(s):
-        to = (z + s + 1) % 4
+        to = far(s)
         return (q.at[:, al(2 * to + 1, WIDE)], qrel.at[z], s_qr.at[s], r_qrel.at[z], to * 4 + x, h)
 
     def copy_qo():
@@ -121,27 +125,28 @@
         return (q.at[:, al(to, WIDE)], qbuf.at[h], s_qa.at[s], r_q.at[h], c, to)
 
     def copy_qf(s):
-        src = (z + 3 - s) % 4
+        src = (y + z + s) % 4
         return (qrel.at[src], qbuf.at[h], s_qf.at[s], r_q.at[h], c, 2 * src + 1)
 
     def copy_g(s):
-        half = s % 2
-        kk = (h + s // 2) % NHEAD
+        half = (s // 2 + x) % 2
+        step = s // 4
+        kk = jnp.where(s % 2 == 0, 2 * ((y + z + step) % 4), 2 * ((z + step) % 4) + 1)
         src = g.at[al(half, PIECE), al(kk, WIDE)]
         return (src, gbuf.at[c], s_g.at[s], r_g.at[c]) + unit(2 * h + half, kk)
 
     def copy_att_far(s):
-        j = (c + s) % NCTX
+        j = (z + 8 - y - s // 4) % 4 * 4 + (x + s) % 4
         slot = z * 2 + x % 2
         return (stg.at[j], arel.at[slot], s_att.at[s], r_arel.at[slot], j, 2 * y + x // 2)
 
     def copy_att_near(s):
-        j = (c + s) % NCTX
+        j = (z + s // 4) % 4 * 4 + (x + s) % 4
         dst = att_o.at[al(x % 2, PIECE), al(kv, WIDE)]
         return (stg.at[j], dst, s_att.at[s], r_att.at[(x % 2) * 8 + kv], j, 2 * y + x // 2)
 
     def relayed(s):
-        return ((z + 4 - s // 2) % 4) * 2 + s % 2
+        return ((y + z + s // 2) % 4) * 2 + s % 2
 
     def copy_af(s):
         m = relayed(s)
@@ -161,40 +166,58 @@
     copy_hal_k = (dk.at[pl.ds(0, MOST)], hk, s_hal.at[0], r_hal.at[0]) + back
     copy_hal_v = (dv.at[pl.ds(0, MOST)], hv, s_hal.at[1], r_hal.at[1]) + back
 
-    def send_kv(s):
-        start(copy_k(s))
-        start(copy_v(s))
-
-    def send_edge(s):
-        start(copy_hk(s))
-        start(copy_hv(s))
-
-    loop(8, send_kv)
+    load_k = pltpu.make_async_copy(k, kvin.at[0], l_kv.at[0])
+    load_v = pltpu.make_async_copy(v, kvin.at[1], l_kv.at[1])
+    load_k.start()
+    load_v.start()
+
+    def away(s, act, copy):
+        @pl.when(far(s) != z)
+        def _():
+            act(copy(s))
+
+    def others(s, act, copy):
+        @pl.when((y + z + s) % 4 != z)
+        def _():
+            act(copy(s))
+
+    loop(4, lambda s: away(s, start, copy_qr))
+    loop(4, lambda s: start(copy_qa(s)))
+    start(copy_qo())
+    load_k.wait()
+    load_v.wait()
+    for n in range(NHEAD):
+        kvs[n, 0] = kvin[0, :, n * DH : (n + 1) * DH]
+        kvs[n, 1] = kvin[1, :, n * DH : (n + 1) * DH]
+    loop(4, lambda s: away(s, start, copy_kvr))
+    loop(4, lambda s: start(copy_kva(s)))
+    start(copy_kvo())
 
     @pl.when(h >= 6)
     def _():
-        loop(8, send_edge)
-
-    loop(3, lambda s: start(copy_qr(s)))
-    start(copy_qo())
-    loop(4, lambda s: start(copy_qa(s)))
+        loop(8, lambda s: start(copy_edge(s)))
+
+    def pass_on(s):
+        src = (y + z + s) % 4
+
+        @pl.when(src != z)
+        def _():
+            landed(qrel.at[src], r_qrel.at[src])
+            start(copy_qf(s))
+            landed(kvrel.at[src], r_kvrel.at[src])
+            start(copy_kvf(s))
+
+    loop(4, pass_on)
     loop(16, lambda s: start(copy_g(s)))
-
-    def pass_on(s):
-        src = (z + 3 - s) % 4
-        landed(qrel.at[src], r_qrel.at[src])
-        start(copy_qf(s))
-
-    loop(3, pass_on)
 
     dk[...] = jnp.zeros_like(dk)
     dv[...] = jnp.zeros_like(dv)
     starts = docs[...].astype(jnp.float32)
 
-    loop(8, lambda b: landed(qbuf.at[b], r_q.at[b]))
-    loop(16, lambda j: landed(gbuf.at[j], r_g.at[j]))
-    loop(10, lambda n: landed(kraw.at[al(n, BLK)], r_k.at[n]))
-    loop(10, lambda n: landed(vbuf.at[al(n, BLK)], r_v.at[n]))
+    loop(10, lambda n: landed(kvbuf.at[n], r_kv.at[n]))
+    for n in range(10):
+        kraw[n * BLK : (n + 1) * BLK] = kvbuf[n, 0]
+        vbuf[n * BLK : (n + 1) * BLK] = kvbuf[n, 1]
     turned = jnp.dot(kraw[...], sign[...].astype(jnp.bfloat16), preferred_element_type=jnp.float32)
     kcod[...] = (turned * ROOT).astype(jnp.bfloat16)
 
@@ -233,6 +256,7 @@
                 att[2 * b, :, lanes] = out[n * BLK : n * BLK + PIECE]
                 att[2 * b + 1, :, lanes] = out[n * BLK + PIECE : (n + 1) * BLK]
 
+    loop(8, lambda b: landed(qbuf.at[b], r_q.at[b]))
     loop(8, forward)
 
     def fill(j):
@@ -250,6 +274,7 @@
             start(copy_att_near(s))
 
     loop(16, send_att)
+    loop(16, lambda j: landed(gbuf.at[j], r_g.at[j]))
 
     def where_from(piece):
         def look(j, found):
@@ -258,7 +283,7 @@
         return lax.fori_loop(0, NCTX, look, 0)
 
     def backward(s):
-        b = (h + s) % NHEAD
+        b = (2 * (y + z) + s) % NHEAD
         j0 = where_from(2 * b)
         j1 = where_from(2 * b + 1)
         rows = pl.ds(pl.multiple_of(b * BLK, BLK), WIN)
@@ -288,15 +313,17 @@
                 dqs[b, :, lanes] = dq[n * BLK : (n + 1) * BLK]
         dk[rows, :] += dk_sum
         dv[rows, :] += dv_sum
+        start(copy_qg(b))
 
     def pass_att(s):
         m = relayed(s)
         landed(arel.at[m], r_arel.at[m])
         start(copy_af(s))
 
-    loop(8, backward)
-    loop(8, pass_att)
-    loop(8, lambda b: start(copy_qg(b)))
+    loop(4, backward)
+    loop(4, pass_att)
+    loop(4, lambda n: backward(n + 4))
+    loop(4, lambda n: pass_att(n + 4))
 
     start(copy_hal_k)
     start(copy_hal_v)
@@ -321,26 +348,21 @@
         start(copy_kg(b))
         start(copy_vg(b))
 
-    loop(8, send_kvg)
-
-    def drain_kv(s):
-        drain(copy_k(s))
-        drain(copy_v(s))
-
-    def drain_edge(s):
-        drain(copy_hk(s))
-        drain(copy_hv(s))
-
-    loop(8, drain_kv)
+    loop(8, lambda s: send_kvg((2 * (y + z) + s) % NHEAD))
+
+    loop(4, lambda s: away(s, drain, copy_kvr))
+    drain(copy_kvo())
+    loop(4, lambda s: drain(copy_kva(s)))
+    loop(4, lambda s: others(s, drain, copy_kvf))
 
     @pl.when(h >= 6)
     def _():
-        loop(8, drain_edge)
-
-    loop(3, lambda s: drain(copy_qr(s)))
+        loop(8, lambda s: drain(copy_edge(s)))
+
+    loop(4, lambda s: away(s, drain, copy_qr))
     drain(copy_qo())
     loop(4, lambda s: drain(copy_qa(s)))
-    loop(3, lambda s: drain(copy_qf(s)))
+    loop(4, lambda s: others(s, drain, copy_qf))
     loop(16, lambda s: drain(copy_g(s)))
 
     @pl.when(co == 0)
@@ -367,8 +389,16 @@
 
 
 def copy_kernel(*refs):
-    for src, dst in zip(refs[:4], refs[4:]):
-        dst[...] = src[...]
+    sems = refs[-1]
+    copies = []
+    for n in range(4):
+        for part in range(4):
+            rows = pl.ds(part * (BLK // 4), BLK // 4)
+            copies.append(pltpu.make_async_copy(refs[n].at[rows], refs[4 + n].at[rows], sems.at[n, part]))
+    for copy in copies:
+        copy.start()
+    for copy in copies:
+        copy.wait()
 
 
 def local(queries, keys, values, out_grad, doc_starts, piece_order):
@@ -389,6 +419,10 @@
         scratch_shapes=[
             pltpu.VMEM((NHEAD, BLK, WIDE), bf),
             pltpu.VMEM((4, BLK, WIDE), bf),
+            pltpu.VMEM((2, BLK, NHEAD * DH), bf),
+            pltpu.VMEM((NHEAD, 2, BLK, DH), bf),
+            pltpu.VMEM((4, 2, BLK, DH), bf),
+            pltpu.VMEM((10, 2, BLK, DH), bf),
             pltpu.VMEM((ext, DH), bf),
             pltpu.VMEM((ext, DH), bf),
             pltpu.VMEM((ext, DH), bf),
@@ -405,8 +439,8 @@
             pltpu.VMEM((NHEAD, BLK, DH), bf),
             pltpu.VMEM((NHEAD, BLK, DH), bf),
         ]
-        + [dma((n,)) for n in (8, 8, 8, 8, 3, 1, 4, 3, 16, 16, 8, 8, 8, 8, 2)]
-        + [dma((n,)) for n in (10, 10, 8, 4, 16, 8, 16, 8, 8, 8, 2)],
+        + [dma((n,)) for n in (2, 4, 1, 4, 4, 8, 4, 1, 4, 4, 16, 16, 8, 8, 8, 8, 2)]
+        + [dma((n,)) for n in (10, 4, 8, 4, 16, 8, 16, 8, 8, 8, 2)],
         compiler_params=pltpu.CompilerParams(
             has_side_effects=True, vmem_limit_bytes=48 * 1024 * 1024
         ),
@@ -415,14 +449,13 @@
         queries, keys, values, out_grad,
         doc_starts.reshape(1, -1), piece_order, jnp.asarray(sign_grid()),
     )
-    blocks = [pl.BlockSpec((PIECE // 4, a.shape[1]), lambda n: (n, 0)) for a in shapes]
     return tuple(
         pl.pallas_call(
             copy_kernel,
-            grid=(8,),
             out_shape=shapes,
-            in_specs=blocks,
-            out_specs=blocks,
+            in_specs=[vmem] * 4,
+            out_specs=[any_spec] * 4,
+            scratch_shapes=[dma((4, 4))],
             name="place",
         )(*results)
     )

time: 171 us -> 155 us (0.906)
  the two profiles are of different devices: /device:TPU:17 before, /device:TPU:49 now
where the time goes in v2:
time: 155 us
  Pallas kernels  146 us (94%)
  local copies, waits for them, and re-layouts  8.17 us (5%)
    pallas_call x1, Pallas kernels, local(): pl.pallas_call(attention_kernel, out_shape=shapes, in_specs=[any_spec] *...  141 us
    unnamed x18, local copies, waits for them, and re-layouts  8.17 us
    pallas_call x1, Pallas kernels, local(): pl.pallas_call(copy_kernel, out_shape=shapes, in_specs=[vmem] * 4, out_sp...  4.57 us

profile of v2, /device:TPU:49, one launch (start us, length us, event | category | flops | bytes accessed | tf_op | source)
XLA Modules:
  0.0 154.7 jit_solution(17963634294059411513)
XLA Ops:
  0.6 0.0 copy-start.4
  0.6 0.9 copy-done.4
  1.6 0.0 copy-start.5
  1.6 0.9 copy-done.5
  2.5 0.0 copy-start.6
  2.5 0.8 copy-done.6
  3.4 0.0 copy-start.7
  3.4 0.7 copy-done.7
  4.1 0.0 copy-start.8
  4.1 0.7 copy-done.8
  4.8 141.3 %attention.1 = (bf16[128,8192]{1,0:T(8,128)(2,1)S(1)}, bf16[128,8192]{1,0:T(8,128)(2,1)S(1)}, bf16[128,1024]{1,0:T(8,128)(2,1)S(1)}, bf16[128,1024]{1,0:T(8,128)(2,1)S(1)}) custom-call(bf16[128,8192]{1,0:T(8,128)(2,1)} %q.1, bf16[128,1024]{1,0:T(8,128)(2,1)S(1)} %copy-done.4, bf16[128,1024]{1,0:T(8,128)(2,1)S(1)} %copy-done.5, bf16[128,8192]{1,0:T(8,128)(2,1)} %g.1, ...), custom_call_target="tpu_custom_call" | custom-call | tf_op jit(solution)/shard_map/attention/pallas_call | solution.py:414
  146.0 0.0 copy-start
  146.0 1.3 copy-done
  147.4 0.0 copy-start.1
  147.4 1.3 copy-done.1
  148.7 0.0 copy-start.2
  148.7 0.7 copy-done.2
  149.4 0.0 copy-start.3
  149.4 0.7 copy-done.3
  150.1 4.6 %place.1 = (bf16[128,8192]{1,0:T(8,128)(2,1)}, bf16[128,8192]{1,0:T(8,128)(2,1)}, bf16[128,1024]{1,0:T(8,128)(2,1)}, bf16[128,1024]{1,0:T(8,128)(2,1)}) custom-call(bf16[128,8192]{1,0:T(8,128)(2,1)} %copy-done, bf16[128,8192]{1,0:T(8,128)(2,1)} %copy-done.1, bf16[128,1024]{1,0:T(8,128)(2,1)} %copy-done.2, bf16[128,1024]{1,0:T(8,128)(2,1)} %copy-done.3), custom_call_target="tpu_custom_call" | custom-call | tf_op jit(solution)/shard_map/place/pallas_call | solution.py:453
Async XLA Ops:
  0.6 1.0 copy-start.4
  1.6 0.9 copy-start.5
  2.5 0.8 copy-start.6
  3.4 0.7 copy-start.7
  4.1 0.7 copy-start.8
  146.0 1.3 copy-start
  147.4 1.3 copy-start.1
  148.7 0.7 copy-start.2
  149.4 0.7 copy-start.3

commit v3 on v2

--- a/solution.py
+++ b/solution.py
@@ -3,7 +3,6 @@
 
 import jax
 import jax.numpy as jnp
-import numpy as np
 from jax import lax
 from jax.experimental import pallas as pl
 from jax.experimental.pallas import tpu as pltpu
@@ -19,18 +18,20 @@
 WIDE = 1024
 NCTX = 16
 NHEAD = 8
-GROUP = 2
+GROUP = 4
 NEG = -1e30
+MOVES = (
+    (1, 1), (3, 3), (1, 3), (3, 1), (1, 0), (3, 0), (0, 1), (0, 3),
+    (2, 1), (2, 3), (1, 2), (3, 2), (2, 2), (2, 0), (0, 2), (0, 0),
+)
 ROOT = 1.0 / math.sqrt(DH)
 
 
 def sign_grid():
-    ids = np.arange(DH)
-    common = ids[:, None] & ids[None, :]
-    parity = np.zeros((DH, DH), np.int64)
-    for bit in range(8):
-        parity += (common >> bit) & 1
-    return np.where(parity % 2 == 0, 1.0, -1.0).astype(np.float32)
+    common = lax.broadcasted_iota(jnp.int32, (DH, DH), 0) & lax.broadcasted_iota(jnp.int32, (DH, DH), 1)
+    for shift in (4, 2, 1):
+        common = common ^ (common >> shift)
+    return (1 - 2 * (common & 1)).astype(jnp.float32)
 
 
 def unit(shard, kv):
@@ -42,9 +43,9 @@
 
 
 def attention_kernel(
-    q, k, v, g, docs, order, sign,
+    q, k, v, g, docs, order,
     att_o, qg_o, kg_o, vg_o,
-    qbuf, qrel, kvin, kvs, kvrel, kvbuf, kraw, kcod, vbuf, gbuf, pst, att, stg, arel, dqs, dk, dv, hk, hv, kst, vst,
+    qbuf, qrel, kvin, kvs, kvrel, kvbuf, kraw, kcod, vbuf, gbuf, pst, inv, att, stg, arel, dqs, dk, dv, hk, hv, kst, vst,
     l_kv, s_kvr, s_kvo, s_kva, s_kvf, s_edge, s_qr, s_qo, s_qa, s_qf, s_g, s_att, s_af, s_qg, s_kg, s_vg, s_hal,
     r_kv, r_kvrel, r_q, r_qrel, r_g, r_arel, r_att, r_qg, r_kg, r_vg, r_hal,
 ):
@@ -91,8 +92,17 @@
 
         lax.fori_loop(0, count, step, 0)
 
+    def turn(s):
+        return jnp.where(s < 2, 1 + 2 * s, 6 - 2 * s)
+
+    def turn_half(s):
+        return jnp.where(s < 4, 1 + 2 * (s % 2), 2 - 2 * (s % 2)), s // 2 % 2
+
     def far(s):
-        return (z + 8 - y - s) % 4
+        return (z + 8 - y - turn(s)) % 4
+
+    def near(s):
+        return (y + z + turn(s)) % 4
 
     def copy_kvr(s):
         to = far(s)
@@ -102,11 +112,11 @@
         return (kvs.at[2 * z + 1], kvbuf.at[h + 2], s_kvo.at[0], r_kv.at[h + 2], c, 2 * z + 1)
 
     def copy_kva(s):
-        to = 2 * ((y + s) % 4)
+        to = 2 * ((y + turn(s)) % 4)
         return (kvs.at[to], kvbuf.at[h + 2], s_kva.at[s], r_kv.at[h + 2], c, to)
 
     def copy_kvf(s):
-        src = (y + z + s) % 4
+        src = near(s)
         return (kvrel.at[src], kvbuf.at[h + 2], s_kvf.at[s], r_kv.at[h + 2], c, 2 * src + 1)
 
     def copy_edge(s):
@@ -121,32 +131,34 @@
         return (q.at[:, al(2 * z + 1, WIDE)], qbuf.at[h], s_qo.at[0], r_q.at[h], c, 2 * z + 1)
 
     def copy_qa(s):
-        to = 2 * ((y + s) % 4)
+        to = 2 * ((y + turn(s)) % 4)
         return (q.at[:, al(to, WIDE)], qbuf.at[h], s_qa.at[s], r_q.at[h], c, to)
 
     def copy_qf(s):
-        src = (y + z + s) % 4
+        src = near(s)
         return (qrel.at[src], qbuf.at[h], s_qf.at[s], r_q.at[h], c, 2 * src + 1)
 
     def copy_g(s):
-        half = (s // 2 + x) % 2
-        step = s // 4
-        kk = jnp.where(s % 2 == 0, 2 * ((y + z + step) % 4), 2 * ((z + step) % 4) + 1)
+        step, half = turn_half(s % 8)
+        half = (half + x) % 2
+        kk = jnp.where(s >= 8, 2 * ((y + z + step) % 4), 2 * ((z + step) % 4) + 1)
         src = g.at[al(half, PIECE), al(kk, WIDE)]
         return (src, gbuf.at[c], s_g.at[s], r_g.at[c]) + unit(2 * h + half, kk)
 
     def copy_att_far(s):
-        j = (z + 8 - y - s // 4) % 4 * 4 + (x + s) % 4
+        j = (z + 8 - y - MOVES[s][0]) % 4 * 4 + (x + MOVES[s][1]) % 4
         slot = z * 2 + x % 2
         return (stg.at[j], arel.at[slot], s_att.at[s], r_arel.at[slot], j, 2 * y + x // 2)
 
     def copy_att_near(s):
-        j = (z + s // 4) % 4 * 4 + (x + s) % 4
+        j = (z + MOVES[s][0]) % 4 * 4 + (x + MOVES[s][1]) % 4
         dst = att_o.at[al(x % 2, PIECE), al(kv, WIDE)]
         return (stg.at[j], dst, s_att.at[s], r_att.at[(x % 2) * 8 + kv], j, 2 * y + x // 2)
 
     def relayed(s):
-        return ((y + z + s // 2) % 4) * 2 + s % 2
+        step, half = turn_half(s)
+        step = jnp.where(s < 4, step, 2 - step)
+        return ((y + z + step) % 4) * 2 + half
 
     def copy_af(s):
         m = relayed(s)
@@ -177,7 +189,7 @@
             act(copy(s))
 
     def others(s, act, copy):
-        @pl.when((y + z + s) % 4 != z)
+        @pl.when(near(s) != z)
         def _():
             act(copy(s))
 
@@ -198,7 +210,7 @@
         loop(8, lambda s: start(copy_edge(s)))
 
     def pass_on(s):
-        src = (y + z + s) % 4
+        src = near(s)
 
         @pl.when(src != z)
         def _():
@@ -217,8 +229,9 @@
     loop(10, lambda n: landed(kvbuf.at[n], r_kv.at[n]))
     for n in range(10):
         kraw[n * BLK : (n + 1) * BLK] = kvbuf[n, 0]
-        vbuf[n * BLK : (n + 1) * BLK] = kvbuf[n, 1]
-    turned = jnp.dot(kraw[...], sign[...].astype(jnp.bfloat16), preferred_element_type=jnp.float32)
+        vbuf[n * BLK : (n + 1) * BLK, :DH] = kvbuf[n, 1]
+    vbuf[:, DH:] = jnp.ones_like(vbuf[:, DH:])
+    turned = jnp.dot(kraw[...], sign_grid().astype(jnp.bfloat16), preferred_element_type=jnp.float32)
     kcod[...] = (turned * ROOT).astype(jnp.bfloat16)
 
     def pair(block, p):
@@ -246,11 +259,12 @@
             score = lax.dot_general(q2, kwin, dims_nt, preferred_element_type=jnp.float32)
             score = score * (ROOT * math.log2(math.e)) + bias
             top = jnp.max(score, axis=1, keepdims=True)
-            e = jnp.exp2(score - top)
-            total = jnp.sum(e, axis=1, keepdims=True)
-            w = (e * (1.0 / total)).astype(jnp.bfloat16)
+            w = jnp.exp2(score - top).astype(jnp.bfloat16)
             pst[b, p] = w
-            out = jnp.dot(w, vwin, preferred_element_type=jnp.float32).astype(jnp.bfloat16)
+            both = jnp.dot(w, vwin, preferred_element_type=jnp.float32)
+            scale = 1.0 / both[:, DH:]
+            inv[b, p] = scale
+            out = (both[:, :DH] * scale).astype(jnp.bfloat16)
             for n in range(GROUP):
                 lanes = slice((GROUP * p + n) * DH, (GROUP * p + n + 1) * DH)
                 att[2 * b, :, lanes] = out[n * BLK : n * BLK + PIECE]
@@ -273,7 +287,8 @@
         def _():
             start(copy_att_near(s))
 
-    loop(16, send_att)
+    for s in range(16):
+        send_att(s)
     loop(16, lambda j: landed(gbuf.at[j], r_g.at[j]))
 
     def where_from(piece):
@@ -283,12 +298,14 @@
         return lax.fori_loop(0, NCTX, look, 0)
 
     def backward(s):
-        b = (2 * (y + z) + s) % NHEAD
+        step, half = turn_half(s)
+        b = (2 * (y + z + step) + half) % NHEAD
         j0 = where_from(2 * b)
         j1 = where_from(2 * b + 1)
         rows = pl.ds(pl.multiple_of(b * BLK, BLK), WIN)
         kwin = kraw[rows, :]
-        vwin = vbuf[rows, :]
+        vwin = vbuf[rows, :DH]
+        ones = jnp.ones((DH, DH), jnp.bfloat16)
         dk_sum = jnp.zeros((WIN, DH), jnp.float32)
         dv_sum = jnp.zeros((WIN, DH), jnp.float32)
         for p in range(8 // GROUP):
@@ -301,10 +318,15 @@
             q2 = jnp.concatenate(q_parts, axis=0)
             g2 = jnp.concatenate(g_parts, axis=0)
             o2 = jnp.concatenate(o_parts, axis=0)
-            delta = jnp.sum(g2.astype(jnp.float32) * o2.astype(jnp.float32), axis=1, keepdims=True)
+            prod = (g2.astype(jnp.float32) * o2.astype(jnp.float32)).astype(jnp.bfloat16)
+            delta = jnp.dot(prod, ones, preferred_element_type=jnp.float32)
             dprob = lax.dot_general(g2, vwin, dims_nt, preferred_element_type=jnp.float32)
             w = pst[b, p]
-            ds = (w.astype(jnp.float32) * (dprob - delta)).astype(jnp.bfloat16)
+            scale = inv[b, p]
+            scaled = jnp.concatenate([scale] * (WIN // DH), axis=1)
+            delta = jnp.concatenate([delta] * (WIN // DH), axis=1)
+            ds = (w.astype(jnp.float32) * (scaled * (dprob - delta))).astype(jnp.bfloat16)
+            g2 = (g2.astype(jnp.float32) * scale).astype(jnp.bfloat16)
             dq = (jnp.dot(ds, kwin, preferred_element_type=jnp.float32) * ROOT).astype(jnp.bfloat16)
             dk_sum += lax.dot_general(ds, q2, dims_tn, preferred_element_type=jnp.float32)
             dv_sum += lax.dot_general(w, g2, dims_tn, preferred_element_type=jnp.float32)
@@ -320,10 +342,10 @@
         landed(arel.at[m], r_arel.at[m])
         start(copy_af(s))
 
+    loop(4, pass_att)
     loop(4, backward)
-    loop(4, pass_att)
+    loop(4, lambda n: pass_att(n + 4))
     loop(4, lambda n: backward(n + 4))
-    loop(4, lambda n: pass_att(n + 4))
 
     start(copy_hal_k)
     start(copy_hal_v)
@@ -332,7 +354,7 @@
         rows = al(b + 2, BLK)
         back_turned = jnp.dot(
             (dk[rows, :] + k_more) * ROOT,
-            sign[...],
+            sign_grid(),
             precision=lax.Precision.HIGHEST,
             preferred_element_type=jnp.float32,
         )
@@ -367,11 +389,13 @@
 
     @pl.when(co == 0)
     def _():
-        loop(16, lambda s: drain(copy_att_far(s)))
+        for s in range(16):
+            drain(copy_att_far(s))
 
     @pl.when(co == 1)
     def _():
-        loop(16, lambda s: drain(copy_att_near(s)))
+        for s in range(16):
+            drain(copy_att_near(s))
 
     loop(8, lambda s: drain(copy_af(s)))
     loop(8, lambda b: drain(copy_qg(b)))
@@ -386,19 +410,6 @@
 
     loop(16, lambda n: landed(att_o.at[al(n // 8, PIECE), al(n % 8, WIDE)], r_att.at[n]))
     loop(8, due)
-
-
-def copy_kernel(*refs):
-    sems = refs[-1]
-    copies = []
-    for n in range(4):
-        for part in range(4):
-            rows = pl.ds(part * (BLK // 4), BLK // 4)
-            copies.append(pltpu.make_async_copy(refs[n].at[rows], refs[4 + n].at[rows], sems.at[n, part]))
-    for copy in copies:
-        copy.start()
-    for copy in copies:
-        copy.wait()
 
 
 def local(queries, keys, values, out_grad, doc_starts, piece_order):
@@ -414,7 +425,7 @@
     results = pl.pallas_call(
         attention_kernel,
         out_shape=shapes,
-        in_specs=[any_spec] * 4 + [vmem, smem, vmem],
+        in_specs=[any_spec] * 4 + [vmem, smem],
         out_specs=[any_spec] * 4,
         scratch_shapes=[
             pltpu.VMEM((NHEAD, BLK, WIDE), bf),
@@ -425,9 +436,10 @@
             pltpu.VMEM((10, 2, BLK, DH), bf),
             pltpu.VMEM((ext, DH), bf),
             pltpu.VMEM((ext, DH), bf),
-            pltpu.VMEM((ext, DH), bf),
+            pltpu.VMEM((ext, 2 * DH), bf),
             pltpu.VMEM((NCTX, PIECE, WIDE), bf),
             pltpu.VMEM((NHEAD, 8 // GROUP, GROUP * BLK, WIN), bf),
+            pltpu.VMEM((NHEAD, 8 // GROUP, GROUP * BLK, DH), f32),
             pltpu.VMEM((NCTX, PIECE, WIDE), bf),
             pltpu.VMEM((NCTX, PIECE, WIDE), bf),
             pltpu.VMEM((8, PIECE, WIDE), bf),
@@ -447,18 +459,9 @@
         name="attention",
     )(
         queries, keys, values, out_grad,
-        doc_starts.reshape(1, -1), piece_order, jnp.asarray(sign_grid()),
+        doc_starts.reshape(1, -1), piece_order,
     )
-    return tuple(
-        pl.pallas_call(
-            copy_kernel,
-            out_shape=shapes,
-            in_specs=[vmem] * 4,
-            out_specs=[any_spec] * 4,
-            scratch_shapes=[dma((4, 4))],
-            name="place",
-        )(*results)
-    )
+    return tuple(results)
 
 
 def solution(mesh):

time: 155 us -> 133 us (0.86)
  the two profiles are of different devices: /device:TPU:49 before, /device:TPU:63 now
where the time goes in v3:
time: 133 us; the launch traced here: 131 us
  Pallas kernels  123 us (92%)
  local copies, waits for them, and re-layouts  7.31 us (5%)
    pallas_call x1, Pallas kernels, local(): pl.pallas_call(attention_kernel, out_shape=shapes, in_specs=[any_spec] *...  123 us
    unnamed x12, local copies, waits for them, and re-layouts  7.31 us

profile of v3, /device:TPU:63, one launch (start us, length us, event | category | flops | bytes accessed | tf_op | source)
XLA Modules:
  0.0 131.2 jit_solution(11787499637302321876)
XLA Ops:
  0.6 0.0 copy-start
  0.6 0.9 copy-done
  1.6 0.0 copy-start.1
  1.6 0.9 copy-done.1
  2.5 0.0 copy-start.2
  2.5 0.7 copy-done.2
  3.2 0.0 copy-start.3
  3.2 0.7 copy-done.3
  3.9 123.2 %attention.1 = (bf16[128,8192]{1,0:T(8,128)(2,1)S(1)}, bf16[128,8192]{1,0:T(8,128)(2,1)S(1)}, bf16[128,1024]{1,0:T(8,128)(2,1)S(1)}, bf16[128,1024]{1,0:T(8,128)(2,1)S(1)}) custom-call(bf16[128,8192]{1,0:T(8,128)(2,1)} %q.1, bf16[128,1024]{1,0:T(8,128)(2,1)S(1)} %copy-done, bf16[128,1024]{1,0:T(8,128)(2,1)S(1)} %copy-done.1, bf16[128,8192]{1,0:T(8,128)(2,1)} %g.1, ...), custom_call_target="tpu_custom_call" | custom-call | tf_op jit(solution)/shard_map/attention/pallas_call | solution.py:425
  127.1 1.3 %copy.14 = bf16[128,8192]{1,0:T(8,128)(2,1)} copy(bf16[128,8192]{1,0:T(8,128)(2,1)S(1)} %get-tuple-element.8) | data formatting | bytes 4194304
  128.4 1.3 %copy.15 = bf16[128,8192]{1,0:T(8,128)(2,1)} copy(bf16[128,8192]{1,0:T(8,128)(2,1)S(1)} %get-tuple-element.9) | data formatting | bytes 4194304
  129.8 0.7 copy.16
  130.5 0.7 copy.17
Async XLA Ops:
  0.6 1.0 copy-start
  1.6 0.9 copy-start.1
  2.5 0.7 copy-start.2
  3.2 0.7 copy-start.3

commit v4 on v3

--- a/solution.py
+++ b/solution.py
@@ -177,6 +177,16 @@
     back = unit((shard + NCTX - 1) % NCTX, kv)
     copy_hal_k = (dk.at[pl.ds(0, MOST)], hk, s_hal.at[0], r_hal.at[0]) + back
     copy_hal_v = (dv.at[pl.ds(0, MOST)], hv, s_hal.at[1], r_hal.at[1]) + back
+
+    barrier = pltpu.get_barrier_semaphore()
+
+    def greet(t):
+        pl.semaphore_signal(
+            barrier, inc=1, device_id={"ctx": t // NHEAD, "head": t % NHEAD}, device_id_type=MESH
+        )
+
+    loop(NCTX * NHEAD, greet)
+    pl.semaphore_wait(barrier, NCTX * NHEAD)
 
     load_k = pltpu.make_async_copy(k, kvin.at[0], l_kv.at[0])
     load_v = pltpu.make_async_copy(v, kvin.at[1], l_kv.at[1])
@@ -297,9 +307,7 @@
 
         return lax.fori_loop(0, NCTX, look, 0)
 
-    def backward(s):
-        step, half = turn_half(s)
-        b = (2 * (y + z + step) + half) % NHEAD
+    def backward(b):
         j0 = where_from(2 * b)
         j1 = where_from(2 * b + 1)
         rows = pl.ds(pl.multiple_of(b * BLK, BLK), WIN)
@@ -335,6 +343,15 @@
                 dqs[b, :, lanes] = dq[n * BLK : (n + 1) * BLK]
         dk[rows, :] += dk_sum
         dv[rows, :] += dv_sum
+
+    def backward_step(s):
+        step, half = turn_half(s)
+        b = (2 * (y + z + step) + half) % NHEAD
+
+        @pl.when(b >= 2)
+        def _():
+            backward(b)
+
         start(copy_qg(b))
 
     def pass_att(s):
@@ -342,13 +359,14 @@
         landed(arel.at[m], r_arel.at[m])
         start(copy_af(s))
 
-    loop(4, pass_att)
-    loop(4, backward)
-    loop(4, lambda n: pass_att(n + 4))
-    loop(4, lambda n: backward(n + 4))
-
+    loop(2, backward)
     start(copy_hal_k)
     start(copy_hal_v)
+    loop(2, backward_step)
+    loop(4, pass_att)
+    loop(2, lambda n: backward_step(n + 2))
+    loop(4, lambda n: pass_att(n + 4))
+    loop(4, lambda n: backward_step(n + 4))
 
     def finish(b, k_more=0.0, v_more=0.0):
         rows = al(b + 2, BLK)
@@ -454,7 +472,7 @@
         + [dma((n,)) for n in (2, 4, 1, 4, 4, 8, 4, 1, 4, 4, 16, 16, 8, 8, 8, 8, 2)]
         + [dma((n,)) for n in (10, 4, 8, 4, 16, 8, 16, 8, 8, 8, 2)],
         compiler_params=pltpu.CompilerParams(
-            has_side_effects=True, vmem_limit_bytes=48 * 1024 * 1024
+            collective_id=0, has_side_effects=True, vmem_limit_bytes=48 * 1024 * 1024
         ),
         name="attention",
     )(

time: 133 us -> 130 us (0.977)
  Pallas kernels: 123 us -> 121 us
    pallas_call x1, Pallas kernels: 123 us -> 121 us  [local(): pl.pallas_call(attention_kernel, out_shape=shapes, in_specs=[any_spec] *...]
where the time goes in v4:
time: 130 us; the launch traced here: 129 us
  Pallas kernels  121 us (93%)
  local copies, waits for them, and re-layouts  7.31 us (6%)
    pallas_call x1, Pallas kernels, local(): pl.pallas_call(attention_kernel, out_shape=shapes, in_specs=[any_spec] *...  121 us
    unnamed x12, local copies, waits for them, and re-layouts  7.31 us

profile of v4, /device:TPU:63, one launch (start us, length us, event | category | flops | bytes accessed | tf_op | source)
XLA Modules:
  0.0 129.4 jit_solution(7041884284637162093)
XLA Ops:
  0.6 0.0 copy-start
  0.6 0.9 copy-done
  1.6 0.0 copy-start.1
  1.6 0.9 copy-done.1
  2.5 0.0 copy-start.2
  2.5 0.7 copy-done.2
  3.2 0.0 copy-start.3
  3.2 0.7 copy-done.3
  3.9 121.4 %attention.1 = (bf16[128,8192]{1,0:T(8,128)(2,1)S(1)}, bf16[128,8192]{1,0:T(8,128)(2,1)S(1)}, bf16[128,1024]{1,0:T(8,128)(2,1)S(1)}, bf16[128,1024]{1,0:T(8,128)(2,1)S(1)}) custom-call(bf16[128,8192]{1,0:T(8,128)(2,1)} %q.1, bf16[128,1024]{1,0:T(8,128)(2,1)S(1)} %copy-done, bf16[128,1024]{1,0:T(8,128)(2,1)S(1)} %copy-done.1, bf16[128,8192]{1,0:T(8,128)(2,1)} %g.1, ...), custom_call_target="tpu_custom_call" | custom-call | tf_op jit(solution)/shard_map/attention/pallas_call | solution.py:443
  125.4 1.3 %copy.14 = bf16[128,8192]{1,0:T(8,128)(2,1)} copy(bf16[128,8192]{1,0:T(8,128)(2,1)S(1)} %get-tuple-element.8) | data formatting | bytes 4194304
  126.7 1.3 %copy.15 = bf16[128,8192]{1,0:T(8,128)(2,1)} copy(bf16[128,8192]{1,0:T(8,128)(2,1)S(1)} %get-tuple-element.9) | data formatting | bytes 4194304
  128.0 0.7 copy.16
  128.7 0.7 copy.17
Async XLA Ops:
  0.6 1.0 copy-start
  1.6 0.9 copy-start.1
  2.5 0.7 copy-start.2
  3.2 0.7 copy-start.3

commit v5 on v4

--- a/solution.py
+++ b/solution.py
@@ -45,9 +45,9 @@
 def attention_kernel(
     q, k, v, g, docs, order,
     att_o, qg_o, kg_o, vg_o,
-    qbuf, qrel, kvin, kvs, kvrel, kvbuf, kraw, kcod, vbuf, gbuf, pst, inv, att, stg, arel, dqs, dk, dv, hk, hv, kst, vst,
-    l_kv, s_kvr, s_kvo, s_kva, s_kvf, s_edge, s_qr, s_qo, s_qa, s_qf, s_g, s_att, s_af, s_qg, s_kg, s_vg, s_hal,
-    r_kv, r_kvrel, r_q, r_qrel, r_g, r_arel, r_att, r_qg, r_kg, r_vg, r_hal,
+    qbuf, qrel, kvs, kvrel, kvbuf, kraw, kcod, vbuf, gbuf, pst, inv, att, stg, arel, dqs, dk, dv, hk, hv, kvst, kvland,
+    s_kvr, s_kvo, s_kva, s_kvf, s_edge, s_qr, s_qo, s_qa, s_qf, s_g, s_att, s_af, s_qg, s_kg, s_hal,
+    r_kv, r_kvrel, r_q, r_qrel, r_g, r_arel, r_att, r_qg, r_kg, r_hal,
 ):
     c = lax.axis_index("ctx")
     h = lax.axis_index("head")
@@ -169,10 +169,7 @@
         return (dqs.at[b], qg_o.at[:, al(kv, WIDE)], s_qg.at[b], r_qg.at[kv], shard, b)
 
     def copy_kg(b):
-        return (kst.at[b], kg_o.at[:, al(kv, DH)], s_kg.at[b], r_kg.at[kv], shard, b)
-
-    def copy_vg(b):
-        return (vst.at[b], vg_o.at[:, al(kv, DH)], s_vg.at[b], r_vg.at[kv], shard, b)
+        return (kvst.at[b], kvland.at[kv], s_kg.at[b], r_kg.at[kv], shard, b)
 
     back = unit((shard + NCTX - 1) % NCTX, kv)
     copy_hal_k = (dk.at[pl.ds(0, MOST)], hk, s_hal.at[0], r_hal.at[0]) + back
@@ -186,12 +183,13 @@
         )
 
     loop(NCTX * NHEAD, greet)
+    for n in range(NHEAD):
+        kvs[n, 0] = k[:, n * DH : (n + 1) * DH]
+        kvs[n, 1] = v[:, n * DH : (n + 1) * DH]
+    dk[...] = jnp.zeros_like(dk)
+    dv[...] = jnp.zeros_like(dv)
+    vbuf[:, DH:] = jnp.ones_like(vbuf[:, DH:])
     pl.semaphore_wait(barrier, NCTX * NHEAD)
-
-    load_k = pltpu.make_async_copy(k, kvin.at[0], l_kv.at[0])
-    load_v = pltpu.make_async_copy(v, kvin.at[1], l_kv.at[1])
-    load_k.start()
-    load_v.start()
 
     def away(s, act, copy):
         @pl.when(far(s) != z)
@@ -206,11 +204,6 @@
     loop(4, lambda s: away(s, start, copy_qr))
     loop(4, lambda s: start(copy_qa(s)))
     start(copy_qo())
-    load_k.wait()
-    load_v.wait()
-    for n in range(NHEAD):
-        kvs[n, 0] = kvin[0, :, n * DH : (n + 1) * DH]
-        kvs[n, 1] = kvin[1, :, n * DH : (n + 1) * DH]
     loop(4, lambda s: away(s, start, copy_kvr))
     loop(4, lambda s: start(copy_kva(s)))
     start(copy_kvo())
@@ -232,15 +225,12 @@
     loop(4, pass_on)
     loop(16, lambda s: start(copy_g(s)))
 
-    dk[...] = jnp.zeros_like(dk)
-    dv[...] = jnp.zeros_like(dv)
     starts = docs[...].astype(jnp.float32)
 
     loop(10, lambda n: landed(kvbuf.at[n], r_kv.at[n]))
     for n in range(10):
         kraw[n * BLK : (n + 1) * BLK] = kvbuf[n, 0]
         vbuf[n * BLK : (n + 1) * BLK, :DH] = kvbuf[n, 1]
-    vbuf[:, DH:] = jnp.ones_like(vbuf[:, DH:])
     turned = jnp.dot(kraw[...], sign_grid().astype(jnp.bfloat16), preferred_element_type=jnp.float32)
     kcod[...] = (turned * ROOT).astype(jnp.bfloat16)
 
@@ -362,33 +352,29 @@
     loop(2, backward)
     start(copy_hal_k)
     start(copy_hal_v)
-    loop(2, backward_step)
-    loop(4, pass_att)
-    loop(2, lambda n: backward_step(n + 2))
-    loop(4, lambda n: pass_att(n + 4))
-    loop(4, lambda n: backward_step(n + 4))
-
-    def finish(b, k_more=0.0, v_more=0.0):
-        rows = al(b + 2, BLK)
-        back_turned = jnp.dot(
-            (dk[rows, :] + k_more) * ROOT,
-            sign_grid(),
-            precision=lax.Precision.HIGHEST,
-            preferred_element_type=jnp.float32,
-        )
-        kst[b] = (back_turned * ROOT).astype(jnp.bfloat16)
-        vst[b] = (dv[rows, :] + v_more).astype(jnp.bfloat16)
-
-    loop(6, finish)
+    loop(6, backward_step)
+    loop(8, pass_att)
+    loop(2, lambda n: backward_step(n + 6))
+
     landed(hk, r_hal.at[0])
     landed(hv, r_hal.at[1])
-    loop(2, lambda n: finish(n + 6, hk[al(n, BLK), :], hv[al(n, BLK), :]))
-
-    def send_kvg(b):
-        start(copy_kg(b))
-        start(copy_vg(b))
-
-    loop(8, lambda s: send_kvg((2 * (y + z) + s) % NHEAD))
+    k_sum = dk[pl.ds(MOST, SHARD), :]
+    v_sum = dv[pl.ds(MOST, SHARD), :]
+    inner = SHARD - MOST
+    k_sum = jnp.concatenate([k_sum[:inner], k_sum[inner:] + hk[...]], axis=0)
+    v_sum = jnp.concatenate([v_sum[:inner], v_sum[inner:] + hv[...]], axis=0)
+    k_sum = jnp.dot(
+        k_sum * ROOT,
+        sign_grid(),
+        precision=lax.Precision.HIGHEST,
+        preferred_element_type=jnp.float32,
+    )
+    k_sum = (k_sum * ROOT).astype(jnp.bfloat16)
+    v_sum = v_sum.astype(jnp.bfloat16)
+    for b in range(NHEAD):
+        kvst[b, 0] = k_sum[b * BLK : (b + 1) * BLK]
+        kvst[b, 1] = v_sum[b * BLK : (b + 1) * BLK]
+    loop(8, lambda s: start(copy_kg((2 * (y + z) + s) % NHEAD)))
 
     loop(4, lambda s: away(s, drain, copy_kvr))
     drain(copy_kvo())
@@ -418,16 +404,14 @@
     loop(8, lambda s: drain(copy_af(s)))
     loop(8, lambda b: drain(copy_qg(b)))
     loop(8, lambda b: drain(copy_kg(b)))
-    loop(8, lambda b: drain(copy_vg(b)))
     drain(copy_hal_k)
     drain(copy_hal_v)
-    def due(n):
-        landed(qg_o.at[:, al(n, WIDE)], r_qg.at[n])
-        landed(kg_o.at[:, al(n, DH)], r_kg.at[n])
-        landed(vg_o.at[:, al(n, DH)], r_vg.at[n])
-
+    loop(8, lambda n: landed(kvland.at[n], r_kg.at[n]))
+    for n in range(NHEAD):
+        kg_o[:, n * DH : (n + 1) * DH] = kvland[n, 0]
+        vg_o[:, n * DH : (n + 1) * DH] = kvland[n, 1]
+    loop(8, lambda n: landed(qg_o.at[:, al(n, WIDE)], r_qg.at[n]))
     loop(16, lambda n: landed(att_o.at[al(n // 8, PIECE), al(n % 8, WIDE)], r_att.at[n]))
-    loop(8, due)
 
 
 def local(queries, keys, values, out_grad, doc_starts, piece_order):
@@ -443,12 +427,11 @@
     results = pl.pallas_call(
         attention_kernel,
         out_shape=shapes,
-        in_specs=[any_spec] * 4 + [vmem, smem],
-        out_specs=[any_spec] * 4,
+        in_specs=[any_spec, vmem, vmem, any_spec, vmem, smem],
+        out_specs=[any_spec] * 2 + [vmem] * 2,
         scratch_shapes=[
             pltpu.VMEM((NHEAD, BLK, WIDE), bf),
             pltpu.VMEM((4, BLK, WIDE), bf),
-            pltpu.VMEM((2, BLK, NHEAD * DH), bf),
             pltpu.VMEM((NHEAD, 2, BLK, DH), bf),
             pltpu.VMEM((4, 2, BLK, DH), bf),
             pltpu.VMEM((10, 2, BLK, DH), bf),
@@ -466,11 +449,11 @@
             pltpu.VMEM((ext, DH), f32),
             pltpu.VMEM((MOST, DH), f32),
             pltpu.VMEM((MOST, DH), f32),
-            pltpu.VMEM((NHEAD, BLK, DH), bf),
-            pltpu.VMEM((NHEAD, BLK, DH), bf),
+            pltpu.VMEM((NHEAD, 2, BLK, DH), bf),
+            pltpu.VMEM((NHEAD, 2, BLK, DH), bf),
         ]
-        + [dma((n,)) for n in (2, 4, 1, 4, 4, 8, 4, 1, 4, 4, 16, 16, 8, 8, 8, 8, 2)]
-        + [dma((n,)) for n in (10, 4, 8, 4, 16, 8, 16, 8, 8, 8, 2)],
+        + [dma((n,)) for n in (4, 1, 4, 4, 8, 4, 1, 4, 4, 16, 16, 8, 8, 8, 2)]
+        + [dma((n,)) for n in (10, 4, 8, 4, 16, 8, 16, 8, 8, 2)],
         compiler_params=pltpu.CompilerParams(
             collective_id=0, has_side_effects=True, vmem_limit_bytes=48 * 1024 * 1024
         ),

time: 130 us -> 124 us (0.954)
  the two profiles are of different devices: /device:TPU:63 before, /device:TPU:27 now
where the time goes in v5:
time: 124 us
  Pallas kernels  116 us (94%)
  local copies, waits for them, and re-layouts  7.31 us (6%)
    pallas_call x1, Pallas kernels, local(): pl.pallas_call(attention_kernel, out_shape=shapes, in_specs=[any_spec, vm...  116 us
    unnamed x12, local copies, waits for them, and re-layouts  7.31 us

profile of v5, /device:TPU:27, one launch (start us, length us, event | category | flops | bytes accessed | tf_op | source)
XLA Modules:
  0.0 123.8 jit_solution(14743012766388867407)
XLA Ops:
  0.6 0.0 copy-start
  0.6 0.9 copy-done
  1.6 0.0 copy-start.1
  1.6 0.9 copy-done.1
  2.5 0.0 copy-start.2
  2.5 0.7 copy-done.2
  3.2 0.0 copy-start.3
  3.2 0.7 copy-done.3
  3.9 115.8 %attention.1 = (bf16[128,8192]{1,0:T(8,128)(2,1)S(1)}, bf16[128,8192]{1,0:T(8,128)(2,1)S(1)}, bf16[128,1024]{1,0:T(8,128)(2,1)S(1)}, bf16[128,1024]{1,0:T(8,128)(2,1)S(1)}) custom-call(bf16[128,8192]{1,0:T(8,128)(2,1)} %q.1, bf16[128,1024]{1,0:T(8,128)(2,1)S(1)} %copy-done, bf16[128,1024]{1,0:T(8,128)(2,1)S(1)} %copy-done.1, bf16[128,8192]{1,0:T(8,128)(2,1)} %g.1, ...), custom_call_target="tpu_custom_call" | custom-call | tf_op jit(solution)/shard_map/attention/pallas_call | solution.py:427
  119.7 1.3 %copy.14 = bf16[128,8192]{1,0:T(8,128)(2,1)} copy(bf16[128,8192]{1,0:T(8,128)(2,1)S(1)} %get-tuple-element.8) | data formatting | bytes 4194304
  121.1 1.3 %copy.15 = bf16[128,8192]{1,0:T(8,128)(2,1)} copy(bf16[128,8192]{1,0:T(8,128)(2,1)S(1)} %get-tuple-element.9) | data formatting | bytes 4194304
  122.4 0.7 copy.16
  123.1 0.7 copy.17
Async XLA Ops:
  0.6 1.0 copy-start
  1.6 0.9 copy-start.1
  2.5 0.7 copy-start.2
  3.2 0.7 copy-start.3

commit v6 on v5

--- a/solution.py
+++ b/solution.py
@@ -140,6 +140,7 @@
 
     def copy_g(s):
         step, half = turn_half(s % 8)
+        step = jnp.where(s >= 8, step, 3 - step)
         half = (half + x) % 2
         kk = jnp.where(s >= 8, 2 * ((y + z + step) % 4), 2 * ((z + step) % 4) + 1)
         src = g.at[al(half, PIECE), al(kk, WIDE)]

time: 124 us -> 123 us (level)
  the two profiles are of different devices: /device:TPU:27 before, /device:TPU:63 now
where the time goes in v6:
time: 123 us
  Pallas kernels  115 us (93%)
  local copies, waits for them, and re-layouts  7.31 us (6%)
    pallas_call x1, Pallas kernels, local(): pl.pallas_call(attention_kernel, out_shape=shapes, in_specs=[any_spec, vm...  115 us
    unnamed x12, local copies, waits for them, and re-layouts  7.31 us

profile of v6, /device:TPU:63, one launch (start us, length us, event | category | flops | bytes accessed | tf_op | source)
XLA Modules:
  0.0 122.5 jit_solution(10312648891652678335)
XLA Ops:
  0.6 0.0 copy-start
  0.6 0.9 copy-done
  1.6 0.0 copy-start.1
  1.6 0.9 copy-done.1
  2.5 0.0 copy-start.2
  2.5 0.7 copy-done.2
  3.2 0.0 copy-start.3
  3.2 0.7 copy-done.3
  3.9 114.6 %attention.1 = (bf16[128,8192]{1,0:T(8,128)(2,1)S(1)}, bf16[128,8192]{1,0:T(8,128)(2,1)S(1)}, bf16[128,1024]{1,0:T(8,128)(2,1)S(1)}, bf16[128,1024]{1,0:T(8,128)(2,1)S(1)}) custom-call(bf16[128,8192]{1,0:T(8,128)(2,1)} %q.1, bf16[128,1024]{1,0:T(8,128)(2,1)S(1)} %copy-done, bf16[128,1024]{1,0:T(8,128)(2,1)S(1)} %copy-done.1, bf16[128,8192]{1,0:T(8,128)(2,1)} %g.1, ...), custom_call_target="tpu_custom_call" | custom-call | tf_op jit(solution)/shard_map/attention/pallas_call | solution.py:428
  118.5 1.3 %copy.14 = bf16[128,8192]{1,0:T(8,128)(2,1)} copy(bf16[128,8192]{1,0:T(8,128)(2,1)S(1)} %get-tuple-element.8) | data formatting | bytes 4194304
  119.8 1.3 %copy.15 = bf16[128,8192]{1,0:T(8,128)(2,1)} copy(bf16[128,8192]{1,0:T(8,128)(2,1)S(1)} %get-tuple-element.9) | data formatting | bytes 4194304
  121.1 0.7 copy.16
  121.8 0.7 copy.17
Async XLA Ops:
  0.6 1.0 copy-start
  1.6 0.9 copy-start.1
  2.5 0.7 copy-start.2
  3.2 0.7 copy-start.3
